TPU v7x, 256 devices: a whole 4x4x8 slice. The times are simulated.
256 devices in a mesh: subj: 4 (over z_hi, core), slab: 64 (over z_lo, y, x).
Axes of the slice: x: 4, y: 4, z: 8 (z_hi: 2, z_lo: 4; z = z_hi * 4 + z_lo), core: 2. Of those that a mesh axis runs over, the one named last changes fastest.
Arguments:
- image: bfloat16 [4, 20, 64, 2, 320], P('subj', None, 'slab'), may hold values from -6 to 6
- upstream: float32 [4, 20, 64, 2, 320], P('subj', None, 'slab'), may hold values from -6 to 6
- coil_maps: float32 [4, 2, 8, 64, 2, 320], P('subj', None, None, 'slab'), may hold values from -1.5 to 1.5
- kernel: float32 [10, 10, 64, 2, 320], P(None, None, None, None, 'slab'), may hold values from -0.5 to 5.5, as said below
- w_first: bfloat16 [3, 3, 3, 64, 20], replicated, may hold values from -0.25 to 0.25
- w_second: bfloat16 [3, 3, 3, 64, 64], replicated, may hold values from -0.15625 to 0.15625
- w_third: bfloat16 [3, 3, 3, 64, 64], replicated, may hold values from -0.15625 to 0.15625
- w_fourth: bfloat16 [3, 3, 3, 64, 64], replicated, may hold values from -0.15625 to 0.15625
- w_last: bfloat16 [3, 3, 3, 20, 64], replicated, may hold values from -0.15625 to 0.15625
Outputs:
- image_grad: float32 [4, 20, 64, 2, 320], P('subj', None, 'slab')
- w_first_grad: float32 [3, 3, 3, 64, 20], replicated
- w_second_grad: float32 [3, 3, 3, 64, 64], replicated
- w_third_grad: float32 [3, 3, 3, 64, 64], replicated
- w_fourth_grad: float32 [3, 3, 3, 64, 64], replicated
- w_last_grad: float32 [3, 3, 3, 20, 64], replicated
Inputs may be any that keep to these rules, and one draw needn't show every extreme that they name: kernel[:, :, kz, x, ky] is a symmetric positive definite 10 x 10 matrix at every k-space point.
All inputs are finite; a program needn't handle non-finite values.
Results may differ from a plain program's by a relative error of at most 0.014.
Values may be sent and summed in bfloat16 or wider, within the bound.
A program may use at most 128 MiB of HBM per device.

v0:
```python
import math

import jax
import jax.numpy as jnp
from jax import lax
from jax.sharding import PartitionSpec as P

ETA_STEP = 0.5
PRECISE = lax.Precision.HIGHEST


def padded_2(block, sides, width):
    for axis, dim in sides:
        count = lax.axis_size(axis)
        forward = [(i, i + 1) for i in range(count - 1)]
        backward = [(target, source) for source, target in forward]
        low = lax.ppermute(
            lax.slice_in_dim(block, block.shape[dim] - width, None, axis=dim), axis, forward
        )
        high = lax.ppermute(lax.slice_in_dim(block, 0, width, axis=dim), axis, backward)
        block = jnp.concatenate([low, block, high], axis=dim)
    return block


def silu_slope(pre_act):
    sigmoid = jax.nn.sigmoid(pre_act)
    return sigmoid * (1.0 + pre_act * (1.0 - sigmoid))


def offsets():
    return [(off_z, off_x, off_y) for off_z in range(3) for off_x in range(3) for off_y in range(3)]


def tap_set(padded_z, forward):
    padded = jnp.pad(padded_z, ((0, 0), (0, 0), (1, 1), (1, 1)))
    count_z = padded_z.shape[1] - 2
    count_x = padded_z.shape[2]
    count_y = padded_z.shape[3]
    pieces = []
    for off_z, off_x, off_y in offsets():
        if forward:
            start_z, start_x, start_y = (off_z, off_x, off_y)
        else:
            start_z, start_x, start_y = (2 - off_z, 2 - off_x, 2 - off_y)
        pieces.append(
            padded[
                :,
                start_z : start_z + count_z,
                start_x : start_x + count_x,
                start_y : start_y + count_y,
            ]
        )
    return jnp.stack(pieces)


def planes_in(activation):
    return padded_2(activation, (("slab", 1),), 1)


def planes_back(delta_grad):
    return padded_2(delta_grad, (("slab", 1),), 1)


def dft_tables(length):
    positions = jnp.arange(length, dtype=jnp.int32)
    products = positions[:, None] * positions[None, :] % length
    angles = products.astype(jnp.float32) * (2.0 * math.pi / length)
    scaling = 1.0 / math.sqrt(length)
    return (jnp.cos(angles) * scaling, jnp.sin(angles) * scaling)


def transform(real_part, imag_part, cosine, sine, pattern, inverse):
    real_cos = jnp.einsum(pattern, real_part, cosine, precision=PRECISE)
    real_sin = jnp.einsum(pattern, real_part, sine, precision=PRECISE)
    imag_cos = jnp.einsum(pattern, imag_part, cosine, precision=PRECISE)
    imag_sin = jnp.einsum(pattern, imag_part, sine, precision=PRECISE)
    if inverse:
        return (real_cos - imag_sin, imag_cos + real_sin)
    return (real_cos + imag_sin, imag_cos - real_sin)


def kspace_mix(arrived, kernel_band, cosine_depth, sine_depth):
    depth_real, depth_imag = transform(
        arrived[0], arrived[1], cosine_depth, sine_depth, "crxyz,zk->crxyk", False
    )
    mixed_real = jnp.einsum("rsxyk,csxyk->crxyk", kernel_band, depth_real, precision=PRECISE)
    mixed_imag = jnp.einsum("rsxyk,csxyk->crxyk", kernel_band, depth_imag, precision=PRECISE)
    back_real, back_imag = transform(
        mixed_real, mixed_imag, cosine_depth, sine_depth, "crxyz,zk->crxyk", True
    )
    return jnp.stack((back_real, back_imag))


def normal_operator(field, maps, kernel_band, tables):
    cosine_rows, sine_rows, cosine_depth, sine_depth = tables
    components = field.shape[0] // 2
    vec_real = field[:components][None]
    vec_imag = field[components:][None]
    map_real = maps[0][:, None]
    map_imag = maps[1][:, None]
    coil_real = map_real * vec_real - map_imag * vec_imag
    coil_imag = map_real * vec_imag + map_imag * vec_real
    spec_real, spec_imag = transform(
        coil_real, coil_imag, cosine_rows, sine_rows, "crzxn,nk->crxkz", False
    )
    spectra = jnp.stack((spec_real, spec_imag))
    arrived = lax.all_to_all(spectra, "slab", split_axis=4, concat_axis=5, tiled=True)
    mixed = kspace_mix(arrived, kernel_band, cosine_depth, sine_depth)
    returned = lax.all_to_all(mixed, "slab", split_axis=5, concat_axis=4, tiled=True)
    back_real, back_imag = transform(
        returned[0], returned[1], cosine_rows, sine_rows, "crxnz,nk->crzxk", True
    )
    out_real = jnp.sum(map_real * back_real + map_imag * back_imag, axis=0)
    out_imag = jnp.sum(map_real * back_imag - map_imag * back_real, axis=0)
    return jnp.concatenate((out_real, out_imag), axis=0)


def body(image, upstream, coil_maps, kernel, w_first, w_second, w_third, w_fourth, w_last):
    weights = (w_first, w_second, w_third, w_fourth, w_last)
    weight_taps = [weight.reshape(27, weight.shape[3], weight.shape[4]) for weight in weights]
    cosine_rows, sine_rows = dft_tables(image.shape[4])
    cosine_depth, sine_depth = dft_tables(kernel.shape[2])
    tables = (cosine_rows, sine_rows, cosine_depth, sine_depth)
    kernel_band = jnp.transpose(kernel, (0, 1, 3, 4, 2))
    local_sums = [jnp.zeros(taps.shape, jnp.float32) for taps in weight_taps]
    direct = upstream[0] - ETA_STEP * normal_operator(
        upstream[0], coil_maps[0], kernel_band, tables
    )
    activation = image[0]
    tap_sets = []
    pre_acts = []
    for level in range(5):
        inputs = tap_set(planes_in(activation), True)
        tap_sets.append(inputs)
        if level < 4:
            pre_act = jnp.einsum(
                "toi,tizxy->ozxy", weight_taps[level], inputs, preferred_element_type=jnp.float32
            )
            pre_acts.append(pre_act)
            activation = jax.nn.silu(pre_act).astype(jnp.bfloat16)
    delta_grad = direct.astype(jnp.bfloat16)
    back_grad = direct
    for level in (4, 3, 2, 1, 0):
        local_sums[level] = jnp.einsum(
            "ozxy,tizxy->toi", delta_grad, tap_sets[level], preferred_element_type=jnp.float32
        )
        shifted = tap_set(planes_back(delta_grad), False)
        back_grad = jnp.einsum(
            "toi,tozxy->izxy", weight_taps[level], shifted, preferred_element_type=jnp.float32
        )
        if level > 0:
            delta_grad = (back_grad * silu_slope(pre_acts[level - 1])).astype(jnp.bfloat16)
    image_grads = [direct + back_grad]
    local_tuple = (local_sums[0], local_sums[1], local_sums[2], local_sums[3], local_sums[4])
    summed = lax.psum(
        (local_tuple[0], local_tuple[1], local_tuple[2], local_tuple[3], local_tuple[4]),
        ("subj", "slab"),
    )
    total_cells = (
        image.shape[0]
        * lax.axis_size("subj")
        * image.shape[2]
        * lax.axis_size("slab")
        * image.shape[3]
        * image.shape[4]
    )
    scaling = 1.0 / math.sqrt(total_cells)
    results = [summed[level].reshape(weights[level].shape) * scaling for level in range(5)]
    return (jnp.stack(image_grads), results[0], results[1], results[2], results[3], results[4])


def solution(mesh):
    in_specs = (
        P("subj", None, "slab", None, None),
        P("subj", None, "slab", None, None),
        P("subj", None, None, "slab", None, None),
        P(None, None, None, None, "slab"),
        P(),
        P(),
        P(),
        P(),
        P(),
    )
    out_specs = (P("subj", None, "slab", None, None), P(), P(), P(), P(), P())
    return jax.shard_map(body, mesh=mesh, in_specs=in_specs, out_specs=out_specs, check_vma=False)
```

profile of v0, /device:TPU:1, one launch (start us, length us, event | category | flops | bytes accessed | tf_op | source)
XLA Modules:
  0.0 623.3 jit_solution(8635704941181876310)
XLA Ops:
  8.6 4.6 collective-permute-start.2
  14.8 2.8 fusion.160
  22.8 4.0 collective-permute-start.4
  26.8 2.8 fusion.162
  33.9 4.5 collective-permute-start.6
  38.3 2.8 fusion.35
  45.4 5.3 collective-permute-start.8
  50.7 2.8 fusion.36
  59.2 6.3 %collective-permute-start.18 = (bf16[64,1,2,320]{3,0,2,1:T(8,128)(2,1)S(1)}, bf16[64,1,2,320]{3,0,2,1:T(8,128)(2,1)S(1)}, u32[]{:S(2)}, u32[]{:S(2)}) collective-permute-start(bf16[64,1,2,320]{3,0,2,1:T(8,128)(2,1)S(1)} %fusion.346), channel_id=1, source_target_pairs={{0,1},{1,2},{2,3},{3,4},{4,5},{5,6},{6,7},{7,8},{8,9},{9,10},{10,1... | collective-permute-start | bytes 245768 | tf_op jit(solution)/shard_map/ppermute | solution.py:17
  65.5 5.0 copy.3471
  70.5 8.8 %reshape.355 = f32[64,1,1600]{2,1,0:T(1,128)} reshape(f32[320,2,1,8,2,10]{5,4,3,2,1,0:T(2,128)} %bitcast.1345) | data formatting | bytes 819200
  79.3 27.8 %all-to-all-start = ((f32[64,1,1600]{2,1,0:T(1,128)}), f32[64,1,1600]{2,1,0:T(1,128)S(1)}, u32[]{:S(2)}, u32[]{:S(2)}) async-start(f32[64,1,1600]{2,1,0:T(1,128)} %reshape.355), calls=%async_computation | async-start | bytes 851968 | tf_op jit(solution)/shard_map/all_to_all | solution.py:107
  107.1 4.2 copy.3476
  128.9 9.9 %reshape.356 = f32[320,2,1,8,2,10]{5,4,3,2,1,0:T(2,128)} reshape(f32[64,1600]{1,0:T(8,128)S(1)} %reduce.2) | data formatting | bytes 819200
  138.8 2.8 copy.3472
  141.6 2.7 fusion.349
  144.4 2.3 copy.3474
  148.3 2.3 copy.3473
  151.4 2.7 convolution_subtract_fusion.1
  154.1 3.1 copy.3478
  157.2 11.8 %convolution_bitcast_fusion = f32[8,10,2,5,64]{1,0,4,3,2:T(8,128)} fusion(f32[8,10,2,5,64]{1,0,4,3,2:T(8,128)} %copy.3478, f32[10,10,2,5,64]{1,0,4,3,2:T(8,128)} %copy.3476), kind=kOutput, calls=%fused_computation.26 | convolution fusion | flops 6144000 | bytes 665600 | tf_op jit(solution)/shard_map/rsxyk,csxyk->crxyk/dot_general | solution.py:87
  169.0 2.3 copy.3480
  174.5 3.1 copy.3475
  177.6 11.6 %convolution_bitcast_fusion.1 = f32[8,10,2,5,64]{1,0,4,3,2:T(8,128)} fusion(f32[8,10,2,5,64]{1,0,4,3,2:T(8,128)} %copy.3475, f32[10,10,2,5,64]{1,0,4,3,2:T(8,128)} %copy.3476), kind=kOutput, calls=%fused_computation.27 | convolution fusion | flops 6144000 | bytes 665600 | tf_op jit(solution)/shard_map/rsxyk,csxyk->crxyk/dot_general | solution.py:86
  189.2 2.7 copy.3477
  194.5 5.9 copy.3483
  200.4 6.7 %reshape.357 = f32[64,1,1600]{2,1,0:T(1,128)} reshape(f32[64,2,2,5,8,10]{5,4,3,2,1,0:T(8,128)} %bitcast.1347) | data formatting | bytes 819200
  207.2 10.2 %all-to-all-start.1 = ((f32[64,1,1600]{2,1,0:T(1,128)}), f32[64,1,1600]{2,1,0:T(1,128)S(1)}, u32[]{:S(2)}, u32[]{:S(2)}) async-start(f32[64,1,1600]{2,1,0:T(1,128)} %reshape.357), calls=%async_computation.1 | async-start | bytes 851968 | tf_op jit(solution)/shard_map/all_to_all | solution.py:109
  220.2 9.1 %all-to-all-done.1 = f32[64,1,1600]{2,1,0:T(1,128)S(1)} async-done(((f32[64,1,1600]{2,1,0:T(1,128)}), f32[64,1,1600]{2,1,0:T(1,128)S(1)}, u32[]{:S(2)}, u32[]{:S(2)}) %all-to-all-start.1) | async-done | bytes 409632 | tf_op jit(solution)/shard_map/all_to_all | solution.py:109
  231.0 7.3 %reshape.358 = f32[64,2,2,5,8,10]{5,4,3,2,1,0:T(8,128)} reshape(f32[64,1600]{1,0:T(8,128)S(1)} %reduce.3) | data formatting | bytes 819200
  238.3 2.8 bitcast_bitcast_fusion
  241.1 1.8 fusion.348
  244.6 2.6 copy.3485
  247.3 2.8 fusion.158
  250.1 3.4 copy.3486
  253.5 2.6 copy.3487
  256.2 2.8 fusion.156
  259.0 2.8 fusion.34
  261.8 3.1 add_reduce_fusion
  266.4 4.0 collective-permute-start
  274.7 4.3 collective-permute-start.10
  280.7 3.6 fusion.37
  288.5 4.0 collective-permute-start.12
  292.5 1.8 fusion.25
  298.4 4.4 collective-permute-start.14
  302.8 1.8 fusion.22
  308.7 5.1 collective-permute-start.16
  318.8 288.1 %all-reduce.13.cloned.1.call-done = (f32[27,64,20]{1,0,2:T(8,128)}, f32[27,64,64]{1,2,0:T(8,128)}, f32[27,64,64]{1,2,0:T(8,128)}, f32[27,64,64]{1,2,0:T(8,128)}, f32[27,20,64]{2,1,0:T(8,128)}) async-done(((f32[27,64,20]{1,0,2:T(8,128)}, f32[27,64,64]{1,2,0:T(8,128)}, f32[27,64,64]{1,2,0:T(8,128)}, f32[27,64,64]{1,2,0:T(8,128)}, f32[27,20,64]{2,1,0:T(8,128)}), (f32[27,64,20]{1,0,2:T(8,128)}, ...) | async-done | bytes 1603600 | tf_op jit(solution)/shard_map/psum | solution.py:155
  (411 shorter events, 86.3 us)
Async XLA Ops:
  7.2 48.5 %copy-start = (bf16[3,3,3,64,64]{4,3,2,1,0:T(8,128)(2,1)S(1)}, bf16[3,3,3,64,64]{4,3,2,1,0:T(8,128)(2,1)}, u32[]{:S(2)}) copy-start(bf16[3,3,3,64,64]{4,3,2,1,0:T(8,128)(2,1)} %param.16) | copy-start | bytes 663556
  7.2 12.6 %copy-start.24 = (bf16[1,20,1,2,320]{4,3,2,1,0:T(2,128)(2,1)S(1)}, bf16[1,20,1,2,320]{4,3,2,1,0:T(2,128)(2,1)}, u32[]{:S(2)}) copy-start(bf16[1,20,1,2,320]{4,3,2,1,0:T(2,128)(2,1)} %param.9) | copy-start | bytes 76804
  7.2 13.9 %copy-start.22 = (bf16[3,3,3,64,20]{3,4,2,1,0:T(8,128)(2,1)S(1)}, bf16[3,3,3,64,20]{3,4,2,1,0:T(8,128)(2,1)}, u32[]{:S(2)}) copy-start(bf16[3,3,3,64,20]{3,4,2,1,0:T(8,128)(2,1)} %param.13) | copy-start | bytes 207364
  7.2 10.4 %collective-permute-start.3 = (bf16[20,1,2,320]{3,2,0,1:T(2,128)(2,1)}, bf16[20,1,2,320]{3,2,0,1:T(2,128)(2,1)S(1)}, u32[]{:S(2)}, u32[]{:S(2)}) collective-permute-start(bf16[20,1,2,320]{3,2,0,1:T(2,128)(2,1)} %bitcast.1381), channel_id=1, source_target_pairs={{1,0},{2,1},{3,2},{4,3},{5,4},{6,5},{7,6},{8,7},{9,8},{10,9},{11,1... | collective-permute-start | bytes 76808 | tf_op jit(solution)/shard_map/ppermute | solution.py:20
  8.6 9.0 %collective-permute-start.2 = (bf16[20,1,2,320]{3,2,0,1:T(2,128)(2,1)}, bf16[20,1,2,320]{3,2,0,1:T(2,128)(2,1)S(1)}, u32[]{:S(2)}, u32[]{:S(2)}) collective-permute-start(bf16[20,1,2,320]{3,2,0,1:T(2,128)(2,1)} %bitcast.1382), channel_id=1, source_target_pairs={{0,1},{1,2},{2,3},{3,4},{4,5},{5,6},{6,7},{7,8},{8,9},{9,10},{10,1... | collective-permute-start | bytes 76808 | tf_op jit(solution)/shard_map/ppermute | solution.py:17
  21.1 8.6 %copy-start.10 = (bf16[27,20,1,2,320]{4,3,1,2,0:T(2,128)(2,1)}, bf16[27,20,1,2,320]{4,3,1,2,0:T(2,128)(2,1)S(1)}, u32[]{:S(2)}) copy-start(bf16[27,20,1,2,320]{4,3,1,2,0:T(2,128)(2,1)S(1)} %constant_dynamic-update-slice_fusion.27) | copy-start | bytes 2073604
  21.5 9.3 %copy-start.14 = (f32[64,2,320]{2,0,1:T(8,128)}, f32[64,2,320]{2,0,1:T(8,128)S(1)}, u32[]{:S(2)}) copy-start(f32[64,2,320]{2,0,1:T(8,128)S(1)} %convolution_bitcast_fusion.3) | copy-start | bytes 491524
  21.5 8.1 %collective-permute-start.5 = (bf16[64,1,2,320]{3,0,2,1:T(8,128)(2,1)S(1)}, bf16[64,1,2,320]{3,0,2,1:T(8,128)(2,1)S(1)}, u32[]{:S(2)}, u32[]{:S(2)}) collective-permute-start(bf16[64,1,2,320]{3,0,2,1:T(8,128)(2,1)S(1)} %fusion.343), channel_id=1, source_target_pairs={{1,0},{2,1},{3,2},{4,3},{5,4},{6,5},{7,6},{8,7},{9,8},{10,9},{11,1... | collective-permute-start | bytes 245768 | tf_op jit(solution)/shard_map/ppermute | solution.py:20
  22.8 6.8 %collective-permute-start.4 = (bf16[64,1,2,320]{3,0,2,1:T(8,128)(2,1)S(1)}, bf16[64,1,2,320]{3,0,2,1:T(8,128)(2,1)S(1)}, u32[]{:S(2)}, u32[]{:S(2)}) collective-permute-start(bf16[64,1,2,320]{3,0,2,1:T(8,128)(2,1)S(1)} %fusion.343), channel_id=1, source_target_pairs={{0,1},{1,2},{2,3},{3,4},{4,5},{5,6},{6,7},{7,8},{8,9},{9,10},{10,1... | collective-permute-start | bytes 245768 | tf_op jit(solution)/shard_map/ppermute | solution.py:17
  29.9 2.0 copy-start.19
  31.9 9.3 %copy-start.1 = (bf16[27,64,1,2,320]{4,1,3,2,0:T(8,128)(2,1)}, bf16[27,64,1,2,320]{4,1,3,2,0:T(8,128)(2,1)S(1)}, u32[]{:S(2)}) copy-start(bf16[27,64,1,2,320]{4,1,3,2,0:T(8,128)(2,1)S(1)} %constant_dynamic-update-slice_fusion.54) | copy-start | bytes 6635524
  32.6 8.6 %collective-permute-start.7 = (bf16[64,1,2,320]{3,0,2,1:T(8,128)(2,1)S(1)}, bf16[64,1,2,320]{3,0,2,1:T(8,128)(2,1)S(1)}, u32[]{:S(2)}, u32[]{:S(2)}) collective-permute-start(bf16[64,1,2,320]{3,0,2,1:T(8,128)(2,1)S(1)} %fusion.344), channel_id=1, source_target_pairs={{1,0},{2,1},{3,2},{4,3},{5,4},{6,5},{7,6},{8,7},{9,8},{10,9},{11,1... | collective-permute-start | bytes 245768 | tf_op jit(solution)/shard_map/ppermute | solution.py:20
  33.9 7.3 %collective-permute-start.6 = (bf16[64,1,2,320]{3,0,2,1:T(8,128)(2,1)S(1)}, bf16[64,1,2,320]{3,0,2,1:T(8,128)(2,1)S(1)}, u32[]{:S(2)}, u32[]{:S(2)}) collective-permute-start(bf16[64,1,2,320]{3,0,2,1:T(8,128)(2,1)S(1)} %fusion.344), channel_id=1, source_target_pairs={{0,1},{1,2},{2,3},{3,4},{4,5},{5,6},{6,7},{7,8},{8,9},{9,10},{10,1... | collective-permute-start | bytes 245768 | tf_op jit(solution)/shard_map/ppermute | solution.py:17
  41.4 2.0 copy-start.17
  43.4 10.1 %copy-start.3 = (bf16[27,64,1,2,320]{4,1,3,2,0:T(8,128)(2,1)}, bf16[27,64,1,2,320]{4,1,3,2,0:T(8,128)(2,1)S(1)}, u32[]{:S(2)}) copy-start(bf16[27,64,1,2,320]{4,1,3,2,0:T(8,128)(2,1)S(1)} %constant_dynamic-update-slice_fusion.81) | copy-start | bytes 6635524
  44.1 9.5 %collective-permute-start.9 = (bf16[64,1,2,320]{3,0,2,1:T(8,128)(2,1)S(1)}, bf16[64,1,2,320]{3,0,2,1:T(8,128)(2,1)S(1)}, u32[]{:S(2)}, u32[]{:S(2)}) collective-permute-start(bf16[64,1,2,320]{3,0,2,1:T(8,128)(2,1)S(1)} %fusion.345), channel_id=1, source_target_pairs={{1,0},{2,1},{3,2},{4,3},{5,4},{6,5},{7,6},{8,7},{9,8},{10,9},{11,1... | collective-permute-start | bytes 245768 | tf_op jit(solution)/shard_map/ppermute | solution.py:20
  45.4 8.2 %collective-permute-start.8 = (bf16[64,1,2,320]{3,0,2,1:T(8,128)(2,1)S(1)}, bf16[64,1,2,320]{3,0,2,1:T(8,128)(2,1)S(1)}, u32[]{:S(2)}, u32[]{:S(2)}) collective-permute-start(bf16[64,1,2,320]{3,0,2,1:T(8,128)(2,1)S(1)} %fusion.345), channel_id=1, source_target_pairs={{0,1},{1,2},{2,3},{3,4},{4,5},{5,6},{6,7},{7,8},{8,9},{9,10},{10,1... | collective-permute-start | bytes 245768 | tf_op jit(solution)/shard_map/ppermute | solution.py:17
  57.8 62.6 %copy-start.8 = (f32[64,2,320]{2,0,1:T(8,128)}, f32[64,2,320]{2,0,1:T(8,128)S(1)}, u32[]{:S(2)}) copy-start(f32[64,2,320]{2,0,1:T(8,128)S(1)} %fusion.49) | copy-start | bytes 491524
  57.9 53.4 %collective-permute-start.19 = (bf16[64,1,2,320]{3,0,2,1:T(8,128)(2,1)S(1)}, bf16[64,1,2,320]{3,0,2,1:T(8,128)(2,1)S(1)}, u32[]{:S(2)}, u32[]{:S(2)}) collective-permute-start(bf16[64,1,2,320]{3,0,2,1:T(8,128)(2,1)S(1)} %fusion.346), channel_id=1, source_target_pairs={{1,0},{2,1},{3,2},{4,3},{5,4},{6,5},{7,6},{8,7},{9,8},{10,9},{11,1... | collective-permute-start | bytes 245768 | tf_op jit(solution)/shard_map/ppermute | solution.py:20
  59.2 52.1 %collective-permute-start.18 = (bf16[64,1,2,320]{3,0,2,1:T(8,128)(2,1)S(1)}, bf16[64,1,2,320]{3,0,2,1:T(8,128)(2,1)S(1)}, u32[]{:S(2)}, u32[]{:S(2)}) collective-permute-start(bf16[64,1,2,320]{3,0,2,1:T(8,128)(2,1)S(1)} %fusion.346), channel_id=1, source_target_pairs={{0,1},{1,2},{2,3},{3,4},{4,5},{5,6},{6,7},{7,8},{8,9},{9,10},{10,1... | collective-permute-start | bytes 245768 | tf_op jit(solution)/shard_map/ppermute | solution.py:17
  70.5 36.6 %copy-start.16 = (f32[10,10,64,2,5]{2,3,4,1,0:T(2,128)S(1)}, f32[10,10,64,2,5]{2,3,4,1,0:T(2,128)}, u32[]{:S(2)}) copy-start(f32[10,10,64,2,5]{2,3,4,1,0:T(2,128)} %param.12) | copy-start | bytes 768004
  79.3 47.5 %all-to-all-start = ((f32[64,1,1600]{2,1,0:T(1,128)}), f32[64,1,1600]{2,1,0:T(1,128)S(1)}, u32[]{:S(2)}, u32[]{:S(2)}) async-start(f32[64,1,1600]{2,1,0:T(1,128)} %reshape.355), calls=%async_computation | async-start | bytes 851968 | tf_op jit(solution)/shard_map/all_to_all | solution.py:107
  189.2 3.6 copy-start.7
  207.2 22.1 %all-to-all-start.1 = ((f32[64,1,1600]{2,1,0:T(1,128)}), f32[64,1,1600]{2,1,0:T(1,128)S(1)}, u32[]{:S(2)}, u32[]{:S(2)}) async-start(f32[64,1,1600]{2,1,0:T(1,128)} %reshape.357), calls=%async_computation.1 | async-start | bytes 851968 | tf_op jit(solution)/shard_map/all_to_all | solution.py:109
  217.3 389.6 %all-reduce.13.cloned.1.call-start = ((), (), s32[]{:S(2)}) async-start(), calls=%async_computation.2 | async-start | bytes 6627328 | tf_op jit(solution)/shard_map/psum | solution.py:155
  256.2 8.8 %copy-start.12 = (f32[1,20,1,2,320]{4,3,2,1,0:T(2,128)S(1)}, f32[1,20,1,2,320]{4,3,2,1,0:T(2,128)}, u32[]{:S(2)}) copy-start(f32[1,20,1,2,320]{4,3,2,1,0:T(2,128)} %param.10) | copy-start | bytes 153604
  265.0 8.1 %copy-start.9 = (f32[64,2,320]{2,0,1:T(8,128)S(1)}, f32[64,2,320]{2,0,1:T(8,128)}, u32[]{:S(2)}) copy-start(f32[64,2,320]{2,0,1:T(8,128)} %copy-done.8) | copy-start | bytes 491524
  265.0 8.1 %copy-start.25 = (bf16[3,3,3,20,64]{4,3,2,1,0:T(8,128)(2,1)S(1)}, bf16[3,3,3,20,64]{4,3,2,1,0:T(8,128)(2,1)}, u32[]{:S(2)}) copy-start(bf16[3,3,3,20,64]{4,3,2,1,0:T(8,128)(2,1)} %param.17) | copy-start | bytes 207364
  265.0 6.2 collective-permute-start.1
  266.4 5.0 collective-permute-start
  271.7 7.3 %copy-start.6 = (bf16[27,64,1,2,320]{4,1,3,2,0:T(8,128)(2,1)S(1)}, bf16[27,64,1,2,320]{4,1,3,2,0:T(8,128)(2,1)}, u32[]{:S(2)}) copy-start(bf16[27,64,1,2,320]{4,1,3,2,0:T(8,128)(2,1)} %copy-done.5) | copy-start | bytes 6635524
  273.4 11.0 %collective-permute-start.11 = (bf16[64,1,2,320]{3,0,2,1:T(8,128)(2,1)S(1)}, bf16[64,1,2,320]{3,0,2,1:T(8,128)(2,1)S(1)}, u32[]{:S(2)}, u32[]{:S(2)}) collective-permute-start(bf16[64,1,2,320]{3,0,2,1:T(8,128)(2,1)S(1)} %bitcast.1356), channel_id=1, source_target_pairs={{1,0},{2,1},{3,2},{4,3},{5,4},{6,5},{7,6},{8,7},{9,8},{10,9},{11,1... | collective-permute-start | bytes 245768 | tf_op jit(solution)/shard_map/ppermute | solution.py:20
  274.7 9.7 %collective-permute-start.10 = (bf16[64,1,2,320]{3,0,2,1:T(8,128)(2,1)S(1)}, bf16[64,1,2,320]{3,0,2,1:T(8,128)(2,1)S(1)}, u32[]{:S(2)}, u32[]{:S(2)}) collective-permute-start(bf16[64,1,2,320]{3,0,2,1:T(8,128)(2,1)S(1)} %bitcast.1357), channel_id=1, source_target_pairs={{0,1},{1,2},{2,3},{3,4},{4,5},{5,6},{6,7},{7,8},{8,9},{9,10},{10,1... | collective-permute-start | bytes 245768 | tf_op jit(solution)/shard_map/ppermute | solution.py:17
  286.1 6.4 %copy-start.4 = (bf16[27,64,1,2,320]{4,1,3,2,0:T(8,128)(2,1)S(1)}, bf16[27,64,1,2,320]{4,1,3,2,0:T(8,128)(2,1)}, u32[]{:S(2)}) copy-start(bf16[27,64,1,2,320]{4,1,3,2,0:T(8,128)(2,1)} %copy-done.3) | copy-start | bytes 6635524
  287.2 7.1 %collective-permute-start.13 = (bf16[64,1,2,320]{3,0,2,1:T(8,128)(2,1)S(1)}, bf16[64,1,2,320]{3,0,2,1:T(8,128)(2,1)S(1)}, u32[]{:S(2)}, u32[]{:S(2)}) collective-permute-start(bf16[64,1,2,320]{3,0,2,1:T(8,128)(2,1)S(1)} %bitcast.1359), channel_id=1, source_target_pairs={{1,0},{2,1},{3,2},{4,3},{5,4},{6,5},{7,6},{8,7},{9,8},{10,9},{11,1... | collective-permute-start | bytes 245768 | tf_op jit(solution)/shard_map/ppermute | solution.py:20
  288.5 5.8 collective-permute-start.12
  294.4 2.0 copy-start.18
  296.0 6.9 %copy-start.2 = (bf16[27,64,1,2,320]{4,1,3,2,0:T(8,128)(2,1)S(1)}, bf16[27,64,1,2,320]{4,1,3,2,0:T(8,128)(2,1)}, u32[]{:S(2)}) copy-start(bf16[27,64,1,2,320]{4,1,3,2,0:T(8,128)(2,1)} %copy-done.1) | copy-start | bytes 6635524
  297.1 7.5 %collective-permute-start.15 = (bf16[64,1,2,320]{3,0,2,1:T(8,128)(2,1)S(1)}, bf16[64,1,2,320]{3,0,2,1:T(8,128)(2,1)S(1)}, u32[]{:S(2)}, u32[]{:S(2)}) collective-permute-start(bf16[64,1,2,320]{3,0,2,1:T(8,128)(2,1)S(1)} %bitcast.1362), channel_id=1, source_target_pairs={{1,0},{2,1},{3,2},{4,3},{5,4},{6,5},{7,6},{8,7},{9,8},{10,9},{11,1... | collective-permute-start | bytes 245768 | tf_op jit(solution)/shard_map/ppermute | solution.py:20
  298.4 6.2 %collective-permute-start.14 = (bf16[64,1,2,320]{3,0,2,1:T(8,128)(2,1)S(1)}, bf16[64,1,2,320]{3,0,2,1:T(8,128)(2,1)S(1)}, u32[]{:S(2)}, u32[]{:S(2)}) collective-permute-start(bf16[64,1,2,320]{3,0,2,1:T(8,128)(2,1)S(1)} %bitcast.1363), channel_id=1, source_target_pairs={{0,1},{1,2},{2,3},{3,4},{4,5},{5,6},{6,7},{7,8},{8,9},{9,10},{10,1... | collective-permute-start | bytes 245768 | tf_op jit(solution)/shard_map/ppermute | solution.py:17
  304.8 2.0 copy-start.15
  304.8 2.0 copy-start.20
  306.3 7.5 %copy-start.11 = (bf16[27,20,1,2,320]{4,3,1,2,0:T(2,128)(2,1)S(1)}, bf16[27,20,1,2,320]{4,3,1,2,0:T(2,128)(2,1)}, u32[]{:S(2)}) copy-start(bf16[27,20,1,2,320]{4,3,1,2,0:T(2,128)(2,1)} %copy-done.10) | copy-start | bytes 2073604
  307.4 7.6 %collective-permute-start.17 = (bf16[64,1,2,320]{3,0,2,1:T(8,128)(2,1)S(1)}, bf16[64,1,2,320]{3,0,2,1:T(8,128)(2,1)S(1)}, u32[]{:S(2)}, u32[]{:S(2)}) collective-permute-start(bf16[64,1,2,320]{3,0,2,1:T(8,128)(2,1)S(1)} %bitcast.1353), channel_id=1, source_target_pairs={{1,0},{2,1},{3,2},{4,3},{5,4},{6,5},{7,6},{8,7},{9,8},{10,9},{11,1... | collective-permute-start | bytes 245768 | tf_op jit(solution)/shard_map/ppermute | solution.py:20
  308.7 6.7 %collective-permute-start.16 = (bf16[64,1,2,320]{3,0,2,1:T(8,128)(2,1)S(1)}, bf16[64,1,2,320]{3,0,2,1:T(8,128)(2,1)S(1)}, u32[]{:S(2)}, u32[]{:S(2)}) collective-permute-start(bf16[64,1,2,320]{3,0,2,1:T(8,128)(2,1)S(1)} %bitcast.1354), channel_id=1, source_target_pairs={{0,1},{1,2},{2,3},{3,4},{4,5},{5,6},{6,7},{7,8},{8,9},{9,10},{10,1... | collective-permute-start | bytes 245768 | tf_op jit(solution)/shard_map/ppermute | solution.py:17
  315.7 2.0 copy-start.23
  607.0 4.4 copy-start.13
  612.8 2.4 copy-start.21
  (1 other events, 1.5 us)
Sparse Core Ops, SparseCore 0:
  315.1 291.7 all-reduce.12
where the time goes:
time: 633 us; the launch traced here: 623 us
  waiting for transfers between devices  298 us (47%)
  local copies, waits for them, and re-layouts  127 us (20%)
  starting transfers between devices  97.7 us (15%)
  matrix products  71.9 us (11%)
  between operations  16.8 us (3%)
  other arithmetic  11.8 us (2%)
    psum x1, waiting for transfers between devices, body(): lax.psum((local_tuple[0], local_tuple[1], local_tuple[2], local_tuple[3],...  288 us
    unnamed x315, local copies, waits for them, and re-layouts  71.1 us
    ppermute x10, starting transfers between devices, padded_2(): lax.ppermute(lax.slice_in_dim(block, block.shape[dim] - width, None, axis...  46.4 us
    all_to_all x1, starting transfers between devices, normal_operator(): lax.all_to_all(spectra, 'slab', split_axis=4, concat_axis=5, tiled=True)  27.8 us
    ppermute x10, starting transfers between devices, padded_2(): lax.ppermute(lax.slice_in_dim(block, 0, width, axis=dim), axis, backward)  13.2 us
  transfers between devices with their start and end apart: 23, of which 4 were waited for; matrix products, arithmetic and copies ran while one was open for 10% of the time, Pallas kernels for 0%

commit v1 on v0

v1 whole, which is shorter than its diff:
```python
import functools
import math

import jax
import jax.numpy as jnp
import ml_dtypes
import numpy as np
from jax import lax
from jax.experimental import pallas as pl
from jax.experimental.pallas import tpu as pltpu
from jax.sharding import PartitionSpec as P

F32 = jnp.float32
BF16 = jnp.bfloat16
MESH = pl.DeviceIdType.MESH
NN = (((1,), (0,)), ((), ()))
NT = (((1,), (1,)), ((), ()))
TN = (((0,), (0,)), ((), ()))
SLABS = 64
NY = 320
NZ = 64
CHUNK = {0: 16, 1: 32, 2: 32, 3: 32, 4: 16}


def lane_of(x, comp, coil):
    group = x * 2 + coil // 4
    base = group * 40 if group < 3 else 128
    return base + comp * 4 + coil % 4


def slot_block(q, j):
    if q < 5:
        return q, j // 2
    if q == 5:
        return j, 1
    return min(3 + j, 4), 1


@functools.lru_cache(None)
def tables():
    half = ml_dtypes.bfloat16
    expand_u = np.zeros((512, 40), np.float32)
    expand_s = np.zeros((512, 32), np.float32)
    collect = np.zeros((512, 128), np.float32)
    for x in range(2):
        for comp in range(10):
            for coil in range(8):
                lane = lane_of(x, comp, coil)
                for part in range(2):
                    expand_u[part * 256 + lane, (part * 10 + comp) * 2 + x] = 1
                    expand_s[part * 256 + lane, part * 16 + coil * 2 + x] = 1
                    collect[part * 256 + lane, x * 64 + part * 10 + comp] = 1
    y = np.arange(NY)
    angle = 2 * np.pi * ((y[:, None] * y[None, :]) % NY) / NY
    cos = (np.cos(angle) / math.sqrt(NY)).reshape(SLABS, 5, NY)
    sin = (np.sin(angle) / math.sqrt(NY)).reshape(SLABS, 5, NY)
    rows = np.zeros((SLABS, 16, 2, 384), np.float32)
    rows[:, 0:10:2, 0, :NY] = cos
    rows[:, 0:10:2, 1, :NY] = sin
    rows[:, 1:10:2, 0, :NY] = -sin
    rows[:, 1:10:2, 1, :NY] = cos
    rows = rows.reshape(1024, 768)
    rows_back = np.zeros((2, NY, SLABS, 16), np.float32)
    cos_t, sin_t = np.moveaxis(cos, 2, 0), np.moveaxis(sin, 2, 0)
    rows_back[0, :, :, 0:10:2] = cos_t
    rows_back[0, :, :, 1:10:2] = -sin_t
    rows_back[1, :, :, 0:10:2] = sin_t
    rows_back[1, :, :, 1:10:2] = cos_t
    rows_back = rows_back.reshape(640, 1024)
    z = np.arange(NZ)
    angle = 2 * np.pi * ((z[:, None] * z[None, :]) % NZ) / NZ
    cos, sin = np.cos(angle) / 8, np.sin(angle) / 8
    depth = np.zeros((7, 2, NZ, NZ, 16), np.float32)
    depth_back = np.zeros((NZ, 16, 7, 2, NZ), np.float32)
    for q in range(7):
        depth[q, 0, :, :, 2 * q] = cos
        depth[q, 0, :, :, 2 * q + 1] = sin
        depth[q, 1, :, :, 2 * q] = -sin
        depth[q, 1, :, :, 2 * q + 1] = cos
        depth_back[:, 2 * q, q, 0] = cos
        depth_back[:, 2 * q, q, 1] = -sin
        depth_back[:, 2 * q + 1, q, 0] = sin
        depth_back[:, 2 * q + 1, q, 1] = cos
    depth = depth.reshape(896, 1024)
    depth_back = depth_back.reshape(1024, 896)
    spread = np.zeros((384, 20, 128), np.float32)
    for shift in range(-9, 10):
        for j in range(3):
            for comp in range(10):
                other = comp + shift
                if 0 <= other < 10:
                    first = j * 40 + comp * 4
                    spread[j * 128 + comp * 10 + other, shift + 9, first : first + 4] = 1
    spread = spread.reshape(384, 2560)
    out = (expand_u, expand_s, collect, rows, rows_back, depth, depth_back, spread)
    return tuple(t.astype(half) for t in out)


def dot(a, b, dims=NN):
    return lax.dot_general(a, b, dims, preferred_element_type=F32)


def shifted(block, step):
    count = block.shape[0]
    row = lax.broadcasted_iota(jnp.int32, block.shape, 0)
    rolled = pltpu.roll(block, step % count, 0)
    keep = row >= step if step > 0 else row < count + step
    return jnp.where(keep, rolled, 0.0)


def main_kernel(
    u_ref, s_ref, up_ref, image_ref, taps_ref, kt_ref, eu_ref, es_ref, eo_ref,
    rows_hbm, rows_back_hbm, depth_hbm, depth_back_hbm, spread_hbm,
    grad_ref, sums_mid_ref, sums_small_ref,
    rows_t, rows_back_t, depth_t, depth_back_t, spread_t,
    coil, maps, message, arrived, mixed, message_back, returned, unpacked, coefs, direct,
    acts, pres, deltas, parts_mid, parts_small, gathered_mid, gathered_small,
    own_mid, own_small, across_mid, across_small, total_mid, total_small,
    table_sem, send_sem, recv_sem, halo_send, halo_recv, sum_send, sum_recv,
):
    subj = lax.axis_index("subj")
    slab = lax.axis_index("slab")
    z_hi, core = subj // 2, subj % 2
    z_lo, place = slab // 16, slab % 16
    plane_index = core * 16 + place
    depth_index = z_hi * 4 + z_lo

    def slab_peer(step):
        return (subj, lax.rem(slab + step, SLABS))

    def plane_peer(step):
        other = lax.rem(plane_index + step, 32)
        return other, (z_hi * 2 + other // 16, z_lo * 16 + other % 16)

    def depth_peer(step):
        other = lax.rem(depth_index + step, 8)
        return other, ((other // 4) * 2 + core, (other % 4) * 16 + place)

    barrier = pltpu.get_barrier_semaphore()

    def greet(device):
        pl.semaphore_signal(barrier, inc=1, device_id=device, device_id_type=MESH)

    @pl.loop(1, SLABS)
    def _(step):
        greet(slab_peer(step))

    @pl.loop(0, 16)
    def _(other):
        greet((z_hi * 2 + 1 - core, z_lo * 16 + other))

    @pl.loop(0, 4)
    def _(other):
        greet(((1 - z_hi) * 2 + core, other * 16 + place))

    fetches = [
        pltpu.make_async_copy(source, target, table_sem.at[i])
        for i, (source, target) in enumerate(
            (
                (rows_hbm, rows_t),
                (spread_hbm, spread_t),
                (depth_hbm, depth_t),
                (depth_back_hbm, depth_back_t),
                (rows_back_hbm, rows_back_t),
            )
        )
    ]
    for fetch in fetches:
        fetch.start()

    zero_plane = jnp.zeros((NY, 128), BF16)
    for side, edge in ((0, 0), (2, SLABS - 1)):

        @pl.when(slab == edge)
        def _(side=side):
            for level in range(5):
                for buffers in (acts, deltas):
                    buffers[level, side] = zero_plane

    for i in range(3):
        parts_mid[i, 28:32] = jnp.zeros((4, 32, 128), BF16)
    for i in range(2):
        parts_small[i, 21:32] = jnp.zeros((11, 16, 128), BF16)
    acts[0, 1] = image_ref[...]

    def halo_copies(buffers, base, level):
        index = base + level
        up = pltpu.make_async_remote_copy(
            buffers.at[level, 1], buffers.at[level, 0],
            halo_send.at[index, 0], halo_recv.at[index, 0],
            (subj, jnp.minimum(slab + 1, SLABS - 1)), MESH,
        )
        down = pltpu.make_async_remote_copy(
            buffers.at[level, 1], buffers.at[level, 2],
            halo_send.at[index, 1], halo_recv.at[index, 1],
            (subj, jnp.maximum(slab - 1, 0)), MESH,
        )
        return up, down

    def halo_start(buffers, base, level):
        up, down = halo_copies(buffers, base, level)

        @pl.when(slab < SLABS - 1)
        def _():
            up.start()

        @pl.when(slab > 0)
        def _():
            down.start()

    def halo_wait(buffers, base, level):
        up, down = halo_copies(buffers, base, level)

        @pl.when(slab < SLABS - 1)
        def _():
            up.wait_send()
            down.wait_recv()

        @pl.when(slab > 0)
        def _():
            down.wait_send()
            up.wait_recv()

    def exchange_start(source, target, which):
        @pl.loop(1, SLABS)
        def _(step):
            subject, other = slab_peer(step)
            pltpu.make_async_remote_copy(
                source.at[other], target.at[slab], send_sem.at[which], recv_sem.at[which],
                (subject, other), MESH,
            ).start()

        target[slab] = source[slab]

    def bulk_wait(buffer, count, semaphore):
        piece = buffer.at[pl.ds(0, count)]
        pltpu.make_async_copy(piece, piece, semaphore).wait()

    def exchange_wait(source, target, which):
        bulk_wait(source, SLABS - 1, send_sem.at[which])
        bulk_wait(target, SLABS - 1, recv_sem.at[which])

    wide_u = dot(eu_ref[...], u_ref[...])
    wide_s = dot(es_ref[...], s_ref[...])
    u_re, u_im = wide_u[:256], wide_u[256:]
    s_re, s_im = wide_s[:256], wide_s[256:]
    coil[...] = jnp.zeros((256, 768), BF16)
    coil[:, 0:NY] = (s_re * u_re - s_im * u_im).astype(BF16)
    coil[:, 384 : 384 + NY] = (s_re * u_im + s_im * u_re).astype(BF16)
    maps[...] = dot(s_ref[...], es_ref[...], (((0,), (1,)), ((), ())))
    fetches[0].wait()
    sub = lax.broadcasted_iota(jnp.int32, (8, 8, 128), 1) // 2

    @pl.loop(0, 8)
    def _(step):
        first = pl.multiple_of(step * 128, 128)
        spectra = dot(rows_t[pl.ds(first, 128), :], coil[...], NT)
        body = spectra[:, :128].reshape(8, 2, 8, 128)
        rest = spectra[:, 128:].reshape(8, 2, 8, 128)
        low, high = rest[:, 0], rest[:, 1]
        lowered = pltpu.roll(low, 6, 1)
        at_one = pltpu.roll(low, 2, 1) + pltpu.roll(low, 40, 2) + pltpu.roll(lowered, 80, 2)
        at_two = lowered + pltpu.roll(pltpu.roll(high, 4, 1), 40, 2)
        extra = jnp.where(sub == 1, at_one, jnp.where(sub == 2, at_two, 0.0))
        packed = jnp.concatenate([body[:, 0:1], (body[:, 1] + extra)[:, None]], axis=1)
        message[pl.ds(step * 8, 8)] = packed.reshape(8, 16, 128).astype(BF16)

    pl.semaphore_wait(barrier, 83)
    halo_start(acts, 0, 0)
    exchange_start(message, arrived, 0)

    def forward(level):
        taps = taps_ref[level]
        wide = [taps[3 * k : 3 * k + 3].reshape(384, 128) for k in range(3)]
        spread_out = dot(acts[level, 1], wide[1], NT)
        halo_wait(acts, 0, level)
        sides = jnp.concatenate([acts[level, 0], acts[level, 2]], axis=1)
        spread_out += dot(sides, jnp.concatenate([wide[0], wide[2]], axis=1), NT)
        pre = (
            shifted(spread_out[:, :128], 1)
            + spread_out[:, 128:256]
            + shifted(spread_out[:, 256:], -1)
        )
        pres[level] = pre
        acts[level + 1, 1] = (pre * jax.nn.sigmoid(pre)).astype(BF16)
        halo_start(acts, 0, level + 1)

    fetches[1].wait()
    blocks = []
    for q in range(7):
        picks = [slot_block(q, j) for j in range(3)]
        blocks.append(jnp.concatenate([kt_ref[ky * 2 + x] for ky, x in picks], axis=1))
    stacked = jnp.concatenate(blocks, axis=0)
    for step in range(10):
        pair = dot(stacked, spread_t[:, step * 256 : step * 256 + 256])
        coefs[2 * step] = pair[:, :128]
        if step < 9:
            coefs[2 * step + 1] = pair[:, 128:]
    forward(0)
    forward(1)

    fetches[2].wait()
    fetches[3].wait()
    exchange_wait(message, arrived, 0)

    @pl.loop(0, 7)
    def _(q):
        first = pl.multiple_of(q * 128, 128)
        spectrum = dot(depth_t[pl.ds(first, 128), :], arrived[...].reshape(1024, 128))
        real, imag = spectrum[:64], spectrum[64:]
        out_real = jnp.zeros((64, 128), F32)
        out_imag = jnp.zeros((64, 128), F32)
        for shift in range(-9, 10):
            factor = coefs[shift + 9, pl.ds(pl.multiple_of(q * 64, 64), 64), :]
            turn = (-4 * shift) % 128
            moved_real = real if turn == 0 else pltpu.roll(real, turn, 1)
            moved_imag = imag if turn == 0 else pltpu.roll(imag, turn, 1)
            out_real += factor * moved_real
            out_imag += factor * moved_imag
        mixed[pl.ds(first, 64), :] = out_real.astype(BF16)
        mixed[pl.ds(first + 64, 64), :] = out_imag.astype(BF16)

    @pl.loop(0, 8)
    def _(step):
        first = pl.multiple_of(step * 128, 128)
        back = dot(depth_back_t[pl.ds(first, 128), :], mixed[...])
        message_back[pl.ds(step * 8, 8)] = back.astype(BF16).reshape(8, 16, 128)

    exchange_start(message_back, returned, 1)
    forward(2)
    forward(3)
    halo_wait(acts, 0, 4)
    exchange_wait(message_back, returned, 1)

    @pl.loop(0, 8)
    def _(step):
        block = returned[pl.ds(step * 8, 8)].astype(F32)
        body = block.reshape(8, 2, 8, 128)[:, 1]
        raised = pltpu.roll(body, 2, 1)
        low = jnp.where(
            sub == 0,
            pltpu.roll(body, 6, 1),
            jnp.where(
                sub == 1,
                pltpu.roll(body, 88, 2),
                jnp.where(sub == 2, pltpu.roll(raised, 48, 2), raised),
            ),
        )
        high = jnp.where(sub == 0, pltpu.roll(pltpu.roll(body, 4, 1), 88, 2), 0.0)
        rest = jnp.concatenate([low[:, None], high[:, None]], axis=1).reshape(128, 128)
        first = pl.multiple_of(step * 128, 128)
        unpacked[pl.ds(first, 128), 0:128] = block.reshape(128, 128).astype(BF16)
        unpacked[pl.ds(first, 128), 128:256] = rest.astype(BF16)

    fetches[4].wait()
    back_re = dot(rows_back_t[0:NY, :], unpacked[...])
    back_im = dot(rows_back_t[NY:, :], unpacked[...])
    s_re, s_im = maps[:, :256], maps[:, 256:]
    out_re = (s_re * back_re + s_im * back_im).astype(BF16)
    out_im = (s_re * back_im - s_im * back_re).astype(BF16)
    normal = dot(out_re, eo_ref[0:256, :]) + dot(out_im, eo_ref[256:, :])
    own_direct = up_ref[...] - 0.5 * normal
    direct[...] = own_direct
    deltas[4, 1] = own_direct.astype(BF16)

    def buffers_of(level):
        if level in (0, 4):
            i = level // 4
            return [
                b.at[i]
                for b in (parts_small, gathered_small, own_small, across_small, total_small)
            ]
        return [
            b.at[level - 1] for b in (parts_mid, gathered_mid, own_mid, across_mid, total_mid)
        ]

    def sum_scatter(level):
        parts, gathered, _, _, _ = buffers_of(level)

        @pl.loop(1, 32)
        def _(step):
            other, device = plane_peer(step)
            pltpu.make_async_remote_copy(
                parts.at[other], gathered.at[plane_index],
                sum_send.at[level, 0], sum_recv.at[level, 0], device, MESH,
            ).start()

        gathered[plane_index] = parts[plane_index]

    def sum_across(level):
        parts, gathered, own, across, _ = buffers_of(level)
        bulk_wait(parts, 31, sum_send.at[level, 0])
        bulk_wait(gathered, 31, sum_recv.at[level, 0])
        own[0] = jnp.sum(gathered[...].astype(F32), axis=0).astype(BF16)

        @pl.loop(1, 8)
        def _(step):
            _, device = depth_peer(step)
            pltpu.make_async_remote_copy(
                own.at[0], across.at[depth_index],
                sum_send.at[level, 1], sum_recv.at[level, 1], device, MESH,
            ).start()

        across[depth_index] = own[0]

    def sum_spread(level):
        _, _, own, across, total = buffers_of(level)
        bulk_wait(across, 7, sum_send.at[level, 1])
        bulk_wait(across, 7, sum_recv.at[level, 1])
        total[plane_index] = jnp.sum(across[...].astype(F32), axis=0).astype(BF16)

        @pl.loop(1, 32)
        def _(step):
            _, device = plane_peer(step)
            pltpu.make_async_remote_copy(
                total.at[plane_index], total.at[plane_index],
                sum_send.at[level, 2], sum_recv.at[level, 2], device, MESH,
            ).start()

    def sum_finish(level):
        total = buffers_of(level)[4]
        bulk_wait(total, 31, sum_send.at[level, 2])
        bulk_wait(total, 31, sum_recv.at[level, 2])
        if level in (0, 4):
            sums_small_ref[level // 4] = total[...].reshape(512, 128)
        else:
            sums_mid_ref[level - 1] = total[...].reshape(1024, 128)

    def weight_part(level, delta):
        parts = buffers_of(level)[0]
        moved = jnp.concatenate(
            [shifted(delta, -1), delta, shifted(delta, 1)], axis=1
        ).astype(BF16)
        inputs = jnp.concatenate([acts[level, 0], acts[level, 1], acts[level, 2]], axis=1)
        if level == 0:
            raw = dot(inputs, moved, TN)
        else:
            raw = dot(moved, inputs, TN)
        count = 24 if level in (0, 4) else 64
        lane = lax.broadcasted_iota(jnp.int32, (count, 128), 1)
        slots, lower, turned = [], [], []
        for a in range(3):
            for b in range(3):
                first = raw[a * 128 : a * 128 + count, b * 128 : b * 128 + 128]
                second = raw[a * 128 + 64 : a * 128 + 64 + count, b * 128 : b * 128 + 128]
                roll = pltpu.roll(second, 64, 1)
                slots.append(first + jnp.where(lane < 64, roll, 0.0))
                lower.append(second)
                turned.append(roll)
        for k in range(5):
            left = lower[2 * k + 1] if k < 4 else jnp.zeros((count, 128), F32)
            slots.append(jnp.where(lane < 64, left, turned[2 * k]))
        if count == 64:
            for k in range(14):
                parts[2 * k : 2 * k + 2] = slots[k].astype(BF16).reshape(2, 32, 128)
        else:
            for k in range(7):
                both = jnp.concatenate([slots[2 * k], slots[2 * k + 1]], axis=0)
                parts[3 * k : 3 * k + 3] = both.astype(BF16).reshape(3, 16, 128)

    halo_start(deltas, 5, 4)
    delta = own_direct.astype(BF16).astype(F32)
    for level in (4, 3, 2, 1, 0):
        weight_part(level, delta)
        sum_scatter(level)
        if level + 2 < 5:
            sum_spread(level + 2)
        if level + 1 < 5:
            sum_across(level + 1)
        taps = taps_ref[level]
        wide = [
            jnp.concatenate([taps[3 * k], taps[3 * k + 1], taps[3 * k + 2]], axis=1)
            for k in (2, 1, 0)
        ]
        spread_out = dot(deltas[level, 1], wide[1])
        halo_wait(deltas, 5, level)
        sides = jnp.concatenate([deltas[level, 0], deltas[level, 2]], axis=1)
        spread_out += dot(sides, jnp.concatenate([wide[0], wide[2]], axis=0))
        back = (
            shifted(spread_out[:, :128], -1)
            + spread_out[:, 128:256]
            + shifted(spread_out[:, 256:], 1)
        )
        if level > 0:
            pre = pres[level - 1]
            sigmoid = jax.nn.sigmoid(pre)
            rounded = (back * (sigmoid * (1.0 + pre * (1.0 - sigmoid)))).astype(BF16)
            deltas[level - 1, 1] = rounded
            halo_start(deltas, 5, level - 1)
            delta = rounded.astype(F32)
        else:
            grad_ref[...] = direct[...] + back
    sum_across(0)
    sum_spread(1)
    sum_spread(0)
    for level in (4, 3, 2, 1, 0):
        sum_finish(level)


def main_call(u, s, up, image, taps, kt):
    eu, es, eo, rows, rows_back, depth, depth_back, spread = tables()
    vmem = pl.BlockSpec(memory_space=pltpu.VMEM)
    hbm = pl.BlockSpec(memory_space=pl.ANY)
    big = [rows, rows_back, depth, depth_back, spread]
    return pl.pallas_call(
        main_kernel,
        out_shape=(
            jax.ShapeDtypeStruct((NY, 128), F32),
            jax.ShapeDtypeStruct((3, 1024, 128), BF16),
            jax.ShapeDtypeStruct((2, 512, 128), BF16),
        ),
        in_specs=[vmem] * 9 + [hbm] * 5,
        out_specs=(vmem, vmem, vmem),
        scratch_shapes=[pltpu.VMEM(t.shape, BF16) for t in big]
        + [
            pltpu.VMEM((256, 768), BF16),
            pltpu.VMEM((NY, 512), F32),
            pltpu.VMEM((SLABS, 16, 128), BF16),
            pltpu.VMEM((SLABS, 16, 128), BF16),
            pltpu.VMEM((896, 128), BF16),
            pltpu.VMEM((SLABS, 16, 128), BF16),
            pltpu.VMEM((SLABS, 16, 128), BF16),
            pltpu.VMEM((1024, 256), BF16),
            pltpu.VMEM((19, 448, 128), F32),
            pltpu.VMEM((NY, 128), F32),
            pltpu.VMEM((5, 3, NY, 128), BF16),
            pltpu.VMEM((4, NY, 128), F32),
            pltpu.VMEM((5, 3, NY, 128), BF16),
            pltpu.VMEM((3, 32, 32, 128), BF16),
            pltpu.VMEM((2, 32, 16, 128), BF16),
            pltpu.VMEM((3, 32, 32, 128), BF16),
            pltpu.VMEM((2, 32, 16, 128), BF16),
            pltpu.VMEM((3, 1, 32, 128), BF16),
            pltpu.VMEM((2, 1, 16, 128), BF16),
            pltpu.VMEM((3, 8, 32, 128), BF16),
            pltpu.VMEM((2, 8, 16, 128), BF16),
            pltpu.VMEM((3, 32, 32, 128), BF16),
            pltpu.VMEM((2, 32, 16, 128), BF16),
            pltpu.SemaphoreType.DMA((5,)),
            pltpu.SemaphoreType.DMA((2,)),
            pltpu.SemaphoreType.DMA((2,)),
            pltpu.SemaphoreType.DMA((10, 2)),
            pltpu.SemaphoreType.DMA((10, 2)),
            pltpu.SemaphoreType.DMA((5, 3)),
            pltpu.SemaphoreType.DMA((5, 3)),
        ],
        compiler_params=pltpu.CompilerParams(
            collective_id=0, has_side_effects=True, vmem_limit_bytes=50 * 1024 * 1024
        ),
        cost_estimate=pl.CostEstimate(
            flops=8_000_000_000, bytes_accessed=20_000_000, transcendentals=400_000
        ),
        name="step",
    )(u, s, up, image, taps, kt, eu, es, eo, rows, rows_back, depth, depth_back, spread)


def finish_kernel(scale, mid_ref, small_ref, first_ref, second_ref, third_ref, fourth_ref, last_ref):
    def place(source, count, keep, target, tap_of):
        def rows_at(slot):
            if count == 64:
                return source[slot * 64 : slot * 64 + 64, :].astype(F32)
            start = (slot // 2) * 48
            both = source[start : start + 48, :].astype(F32)
            return both[(slot % 2) * 24 : (slot % 2) * 24 + 24]

        def left(block):
            return block[:keep, :64] * scale

        def right(block):
            return pltpu.roll(block, 64, 1)[:keep, :64] * scale

        for a in range(3):
            for b in range(3):
                block = rows_at(a * 3 + b)
                target[tap_of(a, b, 0)] = left(block)
                target[tap_of(a, b, 1)] = right(block)
        for k in range(5):
            block = rows_at(9 + k)
            target[tap_of((2 * k) // 3, (2 * k) % 3, 2)] = right(block)
            if k < 4:
                target[tap_of((2 * k + 1) // 3, (2 * k + 1) % 3, 2)] = left(block)

    def usual(a, b, kind):
        return b * 9 + (1, 2, 0)[kind] * 3 + a

    def turned(a, b, kind):
        return a * 9 + (1, 0, 2)[kind] * 3 + b

    place(small_ref.at[0], 24, 20, first_ref, turned)
    place(mid_ref.at[0], 64, 64, second_ref, usual)
    place(mid_ref.at[1], 64, 64, third_ref, usual)
    place(mid_ref.at[2], 64, 64, fourth_ref, usual)
    place(small_ref.at[1], 24, 20, last_ref, usual)


def finish_call(mid, small, cells):
    shapes = [(27, 20, 64), (27, 64, 64), (27, 64, 64), (27, 64, 64), (27, 20, 64)]
    return pl.pallas_call(
        functools.partial(finish_kernel, 1.0 / math.sqrt(cells)),
        out_shape=[jax.ShapeDtypeStruct(shape, F32) for shape in shapes],
        in_specs=[pl.BlockSpec(memory_space=pltpu.VMEM)] * 2,
        out_specs=[pl.BlockSpec(memory_space=pltpu.VMEM)] * 5,
        compiler_params=pltpu.CompilerParams(vmem_limit_bytes=24 * 1024 * 1024),
        name="finish",
    )(mid, small)


def body(image, upstream, coil_maps, kernel, w_first, w_second, w_third, w_fourth, w_last):
    u = upstream[0].reshape(40, NY).astype(BF16)
    s = coil_maps[0].reshape(32, NY).astype(BF16)

    def cells_first(block):
        turned = jnp.transpose(block, (2, 1, 0))
        return jnp.pad(turned, ((0, 0), (0, 0), (0, 44))).reshape(NY, 128)

    up = cells_first(upstream[0, :, 0])
    image_cells = cells_first(image[0, :, 0])
    first = jnp.pad(w_first, ((0, 0),) * 4 + ((0, 44),))
    last = jnp.pad(w_last, ((0, 0),) * 3 + ((0, 44), (0, 0)))
    every = jnp.stack([first, w_second, w_third, w_fourth, last])
    top = jnp.concatenate([every[:, :, 1], every[:, :, 2]], axis=-1)
    bottom = jnp.concatenate([every[:, :, 0], every[:, :, 1]], axis=-1)
    taps = jnp.concatenate([top, bottom], axis=3).reshape(5, 9, 128, 128)
    kt = jnp.transpose(kernel, (4, 3, 2, 0, 1)).astype(BF16).reshape(10, NZ, 100)
    kt = jnp.pad(kt, ((0, 0), (0, 0), (0, 28)))
    grad, mid, small = main_call(u, s, up, image_cells, taps, kt)
    cells = (
        lax.axis_size("subj") * image.shape[0] * lax.axis_size("slab") * image.shape[2] * 2 * NY
    )
    first, second, third, fourth, last = finish_call(mid, small, cells)
    image_grad = jnp.transpose(grad.reshape(NY, 2, 64)[:, :, :20], (2, 1, 0))[None, :, None]
    return (
        image_grad,
        jnp.swapaxes(first, 1, 2).reshape(3, 3, 3, 64, 20),
        second.reshape(3, 3, 3, 64, 64),
        third.reshape(3, 3, 3, 64, 64),
        fourth.reshape(3, 3, 3, 64, 64),
        last.reshape(3, 3, 3, 20, 64),
    )


def solution(mesh):
    in_specs = (
        P("subj", None, "slab", None, None),
        P("subj", None, "slab", None, None),
        P("subj", None, None, "slab", None, None),
        P(None, None, None, None, "slab"),
        P(),
        P(),
        P(),
        P(),
        P(),
    )
    out_specs = (P("subj", None, "slab", None, None), P(), P(), P(), P(), P())
    return jax.shard_map(body, mesh=mesh, in_specs=in_specs, out_specs=out_specs, check_vma=False)
```

time: 633 us -> 105 us (0.17); the launches traced: 623 us -> 105 us
  waiting for transfers between devices: 298 us -> 0 us
  local copies, waits for them, and re-layouts: 127 us -> 5.06 us
  starting transfers between devices: 97.7 us -> 0 us
  Pallas kernels: 0 us -> 97.1 us
  matrix products: 71.9 us -> 0 us
  between operations: 16.8 us -> 0.9 us
  other arithmetic: 11.8 us -> 2.15 us
    psum x1 -> x0, waiting for transfers between devices: 288 us -> none  [body(): lax.psum((local_tuple[0], local_tuple[1], local_tuple[2], local_tuple[3],...]
    pallas_call x0 -> x2, Pallas kernels: none -> 97.1 us  [the longest x1 95.2 us: main_call(): pl.pallas_call(main_kernel, out_shape=(jax.ShapeDtypeStruct((NY, 128), F3...]
    dot_general x32 -> x0, matrix products: 71.9 us -> none  [the longest x1 11.8 us: kspace_mix(): jnp.einsum('rsxyk,csxyk->crxyk', kernel_band, depth_imag, precision=PRECISE)]
    unnamed x315 -> x30, local copies, waits for them, and re-layouts: 71.1 us -> 3.54 us
    ppermute x20 -> x0, starting transfers between devices: 59.6 us -> none  [the longest x10 46.4 us: padded_2(): lax.ppermute(lax.slice_in_dim(block, block.shape[dim] - width, None, axis...]
    all_to_all x2 -> x0, starting transfers between devices: 38 us -> none  [the longest x1 27.8 us: normal_operator(): lax.all_to_all(spectra, 'slab', split_axis=4, concat_axis=5, tiled=True)]
    another operation x16 -> x1, local copies, waits for them, and re-layouts: 17.8 us -> 0.14 us  [body(): every = jnp.stack([first, w_second, w_third, w_fourth, last])]
    slice x6 -> x0, local copies, waits for them, and re-layouts: 14.2 us -> none  [the longest x2 5.02 us: kspace_mix(): arrived[0]]
  transfers between devices with their start and end apart: 23 -> 0, of which waited for: 4 -> 0; matrix products, arithmetic and copies ran while one was open for 10% -> 0% of each run, Pallas kernels for 0% -> 0%
where the time goes in v1:
time: 105 us
  Pallas kernels  97.1 us (92%)
  local copies, waits for them, and re-layouts  5.06 us (5%)
  other arithmetic  2.15 us (2%)
    pallas_call x1, Pallas kernels, main_call(): pl.pallas_call(main_kernel, out_shape=(jax.ShapeDtypeStruct((NY, 128), F3...  95.2 us
    unnamed x30, local copies, waits for them, and re-layouts  3.54 us

profile of v1, /device:TPU:1, one launch (start us, length us, event | category | flops | bytes accessed | tf_op | source)
XLA Modules:
  0.0 105.2 jit_solution(10726848031512316609)
XLA Ops:
  0.6 0.0 copy-start.5
  0.6 0.0 copy-start.6
  0.7 0.0 copy-start.8
  0.7 1.3 %copy.32 = bf16[3,3,3,64,20]{4,3,2,1,0:T(8,128)(2,1)S(1)} copy(bf16[3,3,3,64,20]{3,4,2,1,0:T(8,128)(2,1)} %param.21) | data formatting | bytes 138240 | tf_op args[4]
  1.9 0.1 bitcast_dynamic-update-slice_fusion.4
  2.1 1.1 %bitcast_dynamic-update-slice_fusion.3 = bf16[5,3,3,3,64,64]{5,4,3,2,1,0:T(8,128)(2,1)S(1)} fusion(bf16[5,3,3,3,64,64]{5,4,3,2,1,0:T(8,128)(2,1)S(1)} %bitcast_dynamic-update-slice_fusion.4, bf16[3,3,3,64,64]{4,3,2,1,0:T(8,128)(2,1)} %param.22), kind=kLoop, calls=%fused_computation.7 | loop fusion | bytes 663552
  3.1 0.0 copy-done.5
  3.2 0.1 bitcast_dynamic-update-slice_fusion.2
  3.2 0.0 copy-done.6
  3.2 0.1 bitcast_dynamic-update-slice_fusion.1
  3.3 0.0 copy-done.8
  3.3 0.1 bitcast_dynamic-update-slice_fusion
  3.5 0.4 slice_bitcast_fusion.1
  3.9 0.0 copy-start.4
  3.9 0.0 copy-start.7
  3.9 1.9 %maximum_maximum_fusion = bf16[5,3,3,128,128]{4,3,2,1,0:T(8,128)(2,1)} fusion(bf16[5,3,3,64,64]{4,3,2,1,0:T(8,128)(2,1)S(1)} %get-tuple-element.29, bf16[5,3,3,64,64]{4,3,2,1,0:T(8,128)(2,1)S(1)} %get-tuple-element.30, bf16[5,3,3,64,64]{4,3,2,1,0:T(8,128)(2,1)S(1)} %get-tuple-element.28), kind=kLoop, calls=%fused_computation | loop fusion | flops 5898240 | bytes 2580480 | tf_op jit(solution)/shard_map/concatenate | solution.py:623
  5.9 0.0 copy-start.10
  5.9 0.0 copy-start.9
  5.9 0.0 copy-start
  5.9 0.0 copy-start.1
  5.9 0.0 copy-start.2
  5.9 0.0 copy-start.3
  5.9 0.0 copy-done.4
  5.9 0.2 convert_bitcast_fusion
  6.1 0.1 reshape.54
  6.2 0.3 copy.36
  6.6 0.0 copy-done.7
  6.6 0.1 copy.37.up_ref
  6.8 0.0 copy-done.10
  6.8 0.1 copy.38.image_ref
  7.0 0.0 copy-done.9
  7.1 0.2 copy-done
  7.2 0.0 copy-done.1
  7.2 0.0 copy-done.2
  7.3 0.0 copy-done.3
  7.3 95.2 %step.1 = (f32[320,128]{1,0:T(8,128)S(1)}, bf16[3,1024,128]{2,1,0:T(8,128)(2,1)S(1)}, bf16[2,512,128]{2,1,0:T(8,128)(2,1)S(1)}) custom-call(bf16[40,320]{1,0:T(8,128)(2,1)S(1)} %convert_element_type.27.u_ref, bf16[32,320]{1,0:T(8,128)(2,1)S(1)} %convert_element_type.29.s_ref, f32[320,128]{1,0:T(8,128)S(1)} %copy.37.up_ref, ...), custom_call_target="tpu_custom_call" | custom-call | flops 8000000000 | bytes 20000000 | tf_op jit(solution)/shard_map/step/pallas_call | solution.py:505
  102.5 1.9 %finish.1 = (f32[27,20,64]{2,1,0:T(8,128)}, f32[27,64,64]{2,1,0:T(8,128)}, f32[27,64,64]{2,1,0:T(8,128)}, f32[27,64,64]{2,1,0:T(8,128)}, f32[27,20,64]{2,1,0:T(8,128)}) custom-call(bf16[3,1024,128]{2,1,0:T(8,128)(2,1)S(1)} %get-tuple-element.15.mid_ref, bf16[2,512,128]{2,1,0:T(8,128)(2,1)S(1)} %get-tuple-element.16.small_ref), custom_call_target="tpu_custom_call" | custom-call | tf_op jit(solution)/shard_map/finish/pallas_call | solution.py:598
  104.4 0.1 copy.39
  104.6 0.7 copy.40
  (10 shorter events, 0.2 us)
Async XLA Ops:
  0.6 2.5 %copy-start.5 = (bf16[3,3,3,64,64]{4,3,2,1,0:T(8,128)(2,1)S(1)}, bf16[3,3,3,64,64]{4,3,2,1,0:T(8,128)(2,1)}, u32[]{:S(2)}) copy-start(bf16[3,3,3,64,64]{4,3,2,1,0:T(8,128)(2,1)} %param.23) | copy-start | bytes 663556
  0.6 2.6 %copy-start.6 = (bf16[3,3,3,64,64]{4,3,2,1,0:T(8,128)(2,1)S(1)}, bf16[3,3,3,64,64]{4,3,2,1,0:T(8,128)(2,1)}, u32[]{:S(2)}) copy-start(bf16[3,3,3,64,64]{4,3,2,1,0:T(8,128)(2,1)} %param.24) | copy-start | bytes 663556
  0.7 2.7 %copy-start.8 = (bf16[3,3,3,20,64]{4,3,2,1,0:T(8,128)(2,1)S(1)}, bf16[3,3,3,20,64]{4,3,2,1,0:T(8,128)(2,1)}, u32[]{:S(2)}) copy-start(bf16[3,3,3,20,64]{4,3,2,1,0:T(8,128)(2,1)} %param.25) | copy-start | bytes 207364
  3.9 2.0 %copy-start.4 = (f32[10,10,64,2,5]{2,3,4,1,0:T(2,128)S(1)}, f32[10,10,64,2,5]{2,3,4,1,0:T(2,128)}, u32[]{:S(2)}) copy-start(f32[10,10,64,2,5]{2,3,4,1,0:T(2,128)} %param.20) | copy-start | bytes 768004
  3.9 2.7 %copy-start.7 = (f32[1,20,1,2,320]{4,3,2,1,0:T(2,128)S(1)}, f32[1,20,1,2,320]{4,3,2,1,0:T(2,128)}, u32[]{:S(2)}) copy-start(f32[1,20,1,2,320]{4,3,2,1,0:T(2,128)} %param.18) | copy-start | bytes 153604
  5.9 0.9 copy-start.10
  5.9 1.1 %copy-start.9 = (f32[1,2,8,1,2,320]{5,4,3,2,1,0:T(2,128)S(1)}, f32[1,2,8,1,2,320]{5,4,3,2,1,0:T(2,128)}, u32[]{:S(2)}) copy-start(f32[1,2,8,1,2,320]{5,4,3,2,1,0:T(2,128)} %param.19) | copy-start | bytes 122884
  5.9 1.4 %copy-start = (bf16[640,1024]{1,0:T(8,128)(2,1)S(1)}, bf16[640,1024]{1,0:T(8,128)(2,1)}, u32[]{:S(2)}) copy-start(bf16[640,1024]{1,0:T(8,128)(2,1)} %constant.25.clone.rows_back_hbm) | copy-start | bytes 3932164
  5.9 1.4 %copy-start.1 = (bf16[512,40]{1,0:T(8,128)(2,1)S(1)}, bf16[512,40]{1,0:T(8,128)(2,1)}, u32[]{:S(2)}) copy-start(bf16[512,40]{1,0:T(8,128)(2,1)} %constant.21.clone.eu_ref) | copy-start | bytes 122884
  5.9 1.4 %copy-start.2 = (bf16[512,32]{1,0:T(8,128)(2,1)S(1)}, bf16[512,32]{1,0:T(8,128)(2,1)}, u32[]{:S(2)}) copy-start(bf16[512,32]{1,0:T(8,128)(2,1)} %constant.22.clone.es_ref) | copy-start | bytes 98308
  5.9 1.4 %copy-start.3 = (bf16[512,128]{1,0:T(8,128)(2,1)S(1)}, bf16[512,128]{1,0:T(8,128)(2,1)}, u32[]{:S(2)}) copy-start(bf16[512,128]{1,0:T(8,128)(2,1)} %constant.23.clone.eo_ref) | copy-start | bytes 393220

commit v2 on v1

--- a/solution.py
+++ b/solution.py
@@ -19,7 +19,7 @@
 SLABS = 64
 NY = 320
 NZ = 64
-CHUNK = {0: 16, 1: 32, 2: 32, 3: 32, 4: 16}
+STEP = 8
 
 
 def lane_of(x, comp, coil):
@@ -100,23 +100,17 @@
     return lax.dot_general(a, b, dims, preferred_element_type=F32)
 
 
-def shifted(block, step):
-    count = block.shape[0]
-    row = lax.broadcasted_iota(jnp.int32, block.shape, 0)
-    rolled = pltpu.roll(block, step % count, 0)
-    keep = row >= step if step > 0 else row < count + step
-    return jnp.where(keep, rolled, 0.0)
-
-
 def main_kernel(
-    u_ref, s_ref, up_ref, image_ref, taps_ref, kt_ref, eu_ref, es_ref, eo_ref,
+    u_ref, s_ref, up_ref, image_ref, w1_ref, w2_ref, w3_ref, w4_ref, w5_ref, kt_ref,
+    eu_ref, es_ref, eo_ref,
     rows_hbm, rows_back_hbm, depth_hbm, depth_back_hbm, spread_hbm,
     grad_ref, sums_mid_ref, sums_small_ref,
     rows_t, rows_back_t, depth_t, depth_back_t, spread_t,
-    coil, maps, message, arrived, mixed, message_back, returned, unpacked, coefs, direct,
-    acts, pres, deltas, parts_mid, parts_small, gathered_mid, gathered_small,
+    taps_ref, coil, maps, message, arrived, mixed, message_back, returned, unpacked, coefs, direct,
+    padded, stage_image, stage_delta, acts, slopes, deltas, inside, back_core, back_rows, parts_mid, parts_small, halves_mid, halves_small,
+    folded_mid, folded_small, gathered_mid, gathered_small,
     own_mid, own_small, across_mid, across_small, total_mid, total_small,
-    table_sem, send_sem, recv_sem, halo_send, halo_recv, sum_send, sum_recv,
+    table_sem, send_sem, recv_sem, block_send, block_recv, sum_send, sum_recv,
 ):
     subj = lax.axis_index("subj")
     slab = lax.axis_index("slab")
@@ -129,13 +123,24 @@
         return (subj, lax.rem(slab + step, SLABS))
 
     def plane_peer(step):
-        other = lax.rem(plane_index + step, 32)
-        return other, (z_hi * 2 + other // 16, z_lo * 16 + other % 16)
+        other = lax.rem(place + step, 16)
+        return other, (subj, z_lo * 16 + other)
+
+    twin = (z_hi * 2 + 1 - core, slab)
 
     def depth_peer(step):
         other = lax.rem(depth_index + step, 8)
         return other, ((other // 4) * 2 + core, (other % 4) * 16 + place)
 
+    z_block, y_block = slab // 8, slab % 8
+    zero_planes = jnp.zeros((8, 64, 128), BF16)
+    for first, edge in ((0, 0), (16, 7)):
+
+        @pl.when(z_block == edge)
+        def _(first=first):
+            acts[0, first : first + 8] = zero_planes
+            deltas[4, first : first + 8] = zero_planes
+
     barrier = pltpu.get_barrier_semaphore()
 
     def greet(device):
@@ -145,9 +150,7 @@
     def _(step):
         greet(slab_peer(step))
 
-    @pl.loop(0, 16)
-    def _(other):
-        greet((z_hi * 2 + 1 - core, z_lo * 16 + other))
+    greet(twin)
 
     @pl.loop(0, 4)
     def _(other):
@@ -165,61 +168,52 @@
             )
         )
     ]
-    for fetch in fetches:
-        fetch.start()
-
-    zero_plane = jnp.zeros((NY, 128), BF16)
-    for side, edge in ((0, 0), (2, SLABS - 1)):
-
-        @pl.when(slab == edge)
-        def _(side=side):
-            for level in range(5):
-                for buffers in (acts, deltas):
-                    buffers[level, side] = zero_plane
+    fetches[0].start()
 
     for i in range(3):
         parts_mid[i, 28:32] = jnp.zeros((4, 32, 128), BF16)
     for i in range(2):
         parts_small[i, 21:32] = jnp.zeros((11, 16, 128), BF16)
-    acts[0, 1] = image_ref[...]
-
-    def halo_copies(buffers, base, level):
-        index = base + level
-        up = pltpu.make_async_remote_copy(
-            buffers.at[level, 1], buffers.at[level, 0],
-            halo_send.at[index, 0], halo_recv.at[index, 0],
-            (subj, jnp.minimum(slab + 1, SLABS - 1)), MESH,
-        )
-        down = pltpu.make_async_remote_copy(
-            buffers.at[level, 1], buffers.at[level, 2],
-            halo_send.at[index, 1], halo_recv.at[index, 1],
-            (subj, jnp.maximum(slab - 1, 0)), MESH,
-        )
-        return up, down
-
-    def halo_start(buffers, base, level):
-        up, down = halo_copies(buffers, base, level)
-
-        @pl.when(slab < SLABS - 1)
+    def cut(block, stage):
+        padded[8 : 8 + NY, :] = block
+        for piece in range(8):
+            stage[piece] = padded[40 * piece : 40 * piece + 64, :].astype(BF16)
+
+    padded[0:8, :] = jnp.zeros((8, 128), F32)
+    padded[8 + NY :, :] = jnp.zeros((16, 128), F32)
+    cut(image_ref[...].astype(F32), stage_image)
+
+    def blocks_send(stage, target, which):
+        for group, step in ((1, -1), (2, 1), (0, 0)):
+            other_block = jnp.clip(z_block + step, 0, 7)
+            slot = y_block + 8 - 8 * step
+
+            @pl.when(z_block + step == other_block)
+            def _():
+                @pl.loop(0 if step else 1, 8)
+                def _(turn):
+                    piece = lax.rem(y_block + turn, 8)
+                    pltpu.make_async_remote_copy(
+                        stage.at[piece], target.at[slot],
+                        block_send.at[which, group], block_recv.at[which, group],
+                        (subj, other_block * 8 + piece), MESH,
+                    ).start()
+
+        target[y_block + 8] = stage[y_block]
+
+    def blocks_wait(stage, target, which):
+        bulk_wait(stage, 7, block_send.at[which, 0])
+        bulk_wait(target, 7, block_recv.at[which, 0])
+
+        @pl.when(z_block > 0)
         def _():
-            up.start()
-
-        @pl.when(slab > 0)
+            bulk_wait(stage, 8, block_send.at[which, 1])
+            bulk_wait(target, 8, block_recv.at[which, 2])
+
+        @pl.when(z_block < 7)
         def _():
-            down.start()
-
-    def halo_wait(buffers, base, level):
-        up, down = halo_copies(buffers, base, level)
-
-        @pl.when(slab < SLABS - 1)
-        def _():
-            up.wait_send()
-            down.wait_recv()
-
-        @pl.when(slab > 0)
-        def _():
-            down.wait_send()
-            up.wait_recv()
+            bulk_wait(stage, 8, block_send.at[which, 2])
+            bulk_wait(target, 8, block_recv.at[which, 1])
 
     def exchange_start(source, target, which):
         @pl.loop(1, SLABS)
@@ -249,6 +243,8 @@
     coil[:, 384 : 384 + NY] = (s_re * u_im + s_im * u_re).astype(BF16)
     maps[...] = dot(s_ref[...], es_ref[...], (((0,), (1,)), ((), ())))
     fetches[0].wait()
+    for fetch in fetches[1:]:
+        fetch.start()
     sub = lax.broadcasted_iota(jnp.int32, (8, 8, 128), 1) // 2
 
     @pl.loop(0, 8)
@@ -265,26 +261,61 @@
         packed = jnp.concatenate([body[:, 0:1], (body[:, 1] + extra)[:, None]], axis=1)
         message[pl.ds(step * 8, 8)] = packed.reshape(8, 16, 128).astype(BF16)
 
-    pl.semaphore_wait(barrier, 83)
-    halo_start(acts, 0, 0)
-    exchange_start(message, arrived, 0)
+    slot_z = lax.broadcasted_iota(jnp.int32, (24, 64, 128), 0) + (z_block * 8 - 8)
+    slot_y = lax.broadcasted_iota(jnp.int32, (24, 64, 128), 1) + (y_block * 40 - 8)
+    grid_ok = (slot_z >= 0) & (slot_z < NZ) & (slot_y >= 0) & (slot_y < NY)
+    inside[...] = jnp.where(grid_ok, 1.0, 0.0)
+
+    def three_planes(buffer, first, count):
+        pieces = [buffer[first + k : first + k + count].reshape(count * 64, 128) for k in (-1, 0, 1)]
+        return jnp.concatenate(pieces, axis=1)
+
+    def ranges(low, high):
+        return [(first, min(STEP, high - first)) for first in range(low, high, STEP)]
 
     def forward(level):
         taps = taps_ref[level]
-        wide = [taps[3 * k : 3 * k + 3].reshape(384, 128) for k in range(3)]
-        spread_out = dot(acts[level, 1], wide[1], NT)
-        halo_wait(acts, 0, level)
-        sides = jnp.concatenate([acts[level, 0], acts[level, 2]], axis=1)
-        spread_out += dot(sides, jnp.concatenate([wide[0], wide[2]], axis=1), NT)
-        pre = (
-            shifted(spread_out[:, :128], 1)
-            + spread_out[:, 128:256]
-            + shifted(spread_out[:, 256:], -1)
-        )
-        pres[level] = pre
-        acts[level + 1, 1] = (pre * jax.nn.sigmoid(pre)).astype(BF16)
-        halo_start(acts, 0, level + 1)
-
+        if level == 0:
+            wide = jnp.concatenate(
+                [jnp.concatenate([taps[3 * k + j] for j in range(3)], axis=1) for k in range(3)],
+                axis=0,
+            )
+        else:
+            wide = jnp.concatenate(
+                [taps[3 * k : 3 * k + 3].reshape(384, 128) for k in range(3)], axis=1
+            )
+        for first, count in ranges(level + 1, 23 - level):
+            out = dot(three_planes(acts.at[level], first, count), wide, NN if level == 0 else NT)
+            rows = count * 64
+            pre = (
+                pltpu.roll(out[:, :128], 1, 0)
+                + out[:, 128:256]
+                + pltpu.roll(out[:, 256:], rows - 1, 0)
+            )
+            keep = inside[first : first + count].reshape(rows, 128)
+            sigmoid = jax.nn.sigmoid(pre) * keep
+            value = pre * sigmoid
+            slope = sigmoid + value * (1.0 - jax.nn.sigmoid(pre))
+            acts[level + 1, first : first + count] = value.astype(BF16).reshape(count, 64, 128)
+            slopes[level, first : first + count] = slope.reshape(count, 64, 128)
+
+    for level, w_ref in enumerate((w1_ref, w2_ref, w3_ref, w4_ref, w5_ref)):
+        for tap in range(9):
+            low, middle, high = [
+                w_ref[(tap // 3) * 9 + off_x * 3 + tap % 3].astype(F32) for off_x in range(3)
+            ]
+            if level == 0:
+                low, high = high, low
+            pieces = [jnp.concatenate(pair, axis=1) for pair in ((middle, high), (low, middle))]
+            if level in (0, 4):
+                pieces = [
+                    jnp.concatenate([piece, jnp.zeros((44, 128), F32)], axis=0) for piece in pieces
+                ]
+            taps_ref[level, tap] = jnp.concatenate(pieces, axis=0).astype(BF16)
+
+    pl.semaphore_wait(barrier, 68)
+    exchange_start(message, arrived, 0)
+    blocks_send(stage_image, acts.at[0], 0)
     fetches[1].wait()
     blocks = []
     for q in range(7):
@@ -296,6 +327,7 @@
         coefs[2 * step] = pair[:, :128]
         if step < 9:
             coefs[2 * step + 1] = pair[:, 128:]
+    blocks_wait(stage_image, acts.at[0], 0)
     forward(0)
     forward(1)
 
@@ -329,7 +361,6 @@
     exchange_start(message_back, returned, 1)
     forward(2)
     forward(3)
-    halo_wait(acts, 0, 4)
     exchange_wait(message_back, returned, 1)
 
     @pl.loop(0, 8)
@@ -361,36 +392,51 @@
     normal = dot(out_re, eo_ref[0:256, :]) + dot(out_im, eo_ref[256:, :])
     own_direct = up_ref[...] - 0.5 * normal
     direct[...] = own_direct
-    deltas[4, 1] = own_direct.astype(BF16)
+    cut(own_direct, stage_delta)
+    blocks_send(stage_delta, deltas.at[4], 1)
 
     def buffers_of(level):
         if level in (0, 4):
-            i = level // 4
-            return [
-                b.at[i]
-                for b in (parts_small, gathered_small, own_small, across_small, total_small)
-            ]
-        return [
-            b.at[level - 1] for b in (parts_mid, gathered_mid, own_mid, across_mid, total_mid)
-        ]
+            every = (
+                parts_small, halves_small, folded_small, gathered_small, own_small,
+                across_small, total_small,
+            )
+            return [buffer.at[level // 4] for buffer in every]
+        every = (
+            parts_mid, halves_mid, folded_mid, gathered_mid, own_mid, across_mid, total_mid,
+        )
+        return [buffer.at[level - 1] for buffer in every]
+
+    def halves_copy(level):
+        parts, halves = buffers_of(level)[:2]
+        return pltpu.make_async_remote_copy(
+            parts.at[pl.ds(16 * (1 - core), 16)], halves,
+            sum_send.at[level, 0], sum_recv.at[level, 0], twin, MESH,
+        )
+
+    def sum_halves(level):
+        halves_copy(level).start()
 
     def sum_scatter(level):
-        parts, gathered, _, _, _ = buffers_of(level)
-
-        @pl.loop(1, 32)
+        parts, halves, folded, gathered = buffers_of(level)[:4]
+        halves_copy(level).wait()
+        mine = parts[pl.ds(16 * core, 16)].astype(F32)
+        folded[...] = (mine + halves[...].astype(F32)).astype(BF16)
+
+        @pl.loop(1, 16)
         def _(step):
             other, device = plane_peer(step)
             pltpu.make_async_remote_copy(
-                parts.at[other], gathered.at[plane_index],
-                sum_send.at[level, 0], sum_recv.at[level, 0], device, MESH,
+                folded.at[other], gathered.at[place],
+                sum_send.at[level, 1], sum_recv.at[level, 1], device, MESH,
             ).start()
 
-        gathered[plane_index] = parts[plane_index]
+        gathered[place] = folded[place]
 
     def sum_across(level):
-        parts, gathered, own, across, _ = buffers_of(level)
-        bulk_wait(parts, 31, sum_send.at[level, 0])
-        bulk_wait(gathered, 31, sum_recv.at[level, 0])
+        _, _, folded, gathered, own, across, _ = buffers_of(level)
+        bulk_wait(folded, 15, sum_send.at[level, 1])
+        bulk_wait(gathered, 15, sum_recv.at[level, 1])
         own[0] = jnp.sum(gathered[...].astype(F32), axis=0).astype(BF16)
 
         @pl.loop(1, 8)
@@ -398,40 +444,54 @@
             _, device = depth_peer(step)
             pltpu.make_async_remote_copy(
                 own.at[0], across.at[depth_index],
-                sum_send.at[level, 1], sum_recv.at[level, 1], device, MESH,
+                sum_send.at[level, 2], sum_recv.at[level, 2], device, MESH,
             ).start()
 
         across[depth_index] = own[0]
 
     def sum_spread(level):
-        _, _, own, across, total = buffers_of(level)
-        bulk_wait(across, 7, sum_send.at[level, 1])
-        bulk_wait(across, 7, sum_recv.at[level, 1])
+        across, total = buffers_of(level)[5:]
+        bulk_wait(across, 7, sum_send.at[level, 2])
+        bulk_wait(across, 7, sum_recv.at[level, 2])
         total[plane_index] = jnp.sum(across[...].astype(F32), axis=0).astype(BF16)
 
-        @pl.loop(1, 32)
+        @pl.loop(1, 16)
         def _(step):
             _, device = plane_peer(step)
             pltpu.make_async_remote_copy(
                 total.at[plane_index], total.at[plane_index],
-                sum_send.at[level, 2], sum_recv.at[level, 2], device, MESH,
+                sum_send.at[level, 3], sum_recv.at[level, 3], device, MESH,
             ).start()
 
+    def share_copy(level):
+        half = buffers_of(level)[6].at[pl.ds(16 * core, 16)]
+        return pltpu.make_async_remote_copy(
+            half, half, sum_send.at[level, 4], sum_recv.at[level, 4], twin, MESH
+        )
+
+    def sum_share(level):
+        total = buffers_of(level)[6]
+        bulk_wait(total, 15, sum_send.at[level, 3])
+        bulk_wait(total, 15, sum_recv.at[level, 3])
+        share_copy(level).start()
+
     def sum_finish(level):
-        total = buffers_of(level)[4]
-        bulk_wait(total, 31, sum_send.at[level, 2])
-        bulk_wait(total, 31, sum_recv.at[level, 2])
+        total = buffers_of(level)[6]
+        share_copy(level).wait()
         if level in (0, 4):
             sums_small_ref[level // 4] = total[...].reshape(512, 128)
         else:
             sums_mid_ref[level - 1] = total[...].reshape(1024, 128)
 
-    def weight_part(level, delta):
+    def weight_part(level):
         parts = buffers_of(level)[0]
+        delta = deltas[level, 8:16].astype(F32).reshape(512, 128)
+        row = lax.broadcasted_iota(jnp.int32, (512, 128), 0) % 64
+        delta = jnp.where((row >= 8) & (row < 48), delta, 0.0)
         moved = jnp.concatenate(
-            [shifted(delta, -1), delta, shifted(delta, 1)], axis=1
+            [pltpu.roll(delta, 511, 0), delta, pltpu.roll(delta, 1, 0)], axis=1
         ).astype(BF16)
-        inputs = jnp.concatenate([acts[level, 0], acts[level, 1], acts[level, 2]], axis=1)
+        inputs = three_planes(acts.at[level], 8, 8)
         if level == 0:
             raw = dot(inputs, moved, TN)
         else:
@@ -458,46 +518,64 @@
                 both = jnp.concatenate([slots[2 * k], slots[2 * k + 1]], axis=0)
                 parts[3 * k : 3 * k + 3] = both.astype(BF16).reshape(3, 16, 128)
 
-    halo_start(deltas, 5, 4)
-    delta = own_direct.astype(BF16).astype(F32)
+    blocks_wait(stage_delta, deltas.at[4], 1)
     for level in (4, 3, 2, 1, 0):
-        weight_part(level, delta)
+        weight_part(level)
+        sum_halves(level)
+        taps = taps_ref[level]
+        if level == 0:
+            wide = jnp.concatenate(
+                [jnp.concatenate([taps[3 * k + j] for k in (2, 1, 0)], axis=1) for j in range(3)],
+                axis=0,
+            )
+        else:
+            wide = jnp.concatenate(
+                [jnp.concatenate([taps[3 * k + j] for j in range(3)], axis=1) for k in (2, 1, 0)],
+                axis=0,
+            )
+        for first, count in ranges(8 - level, 16 + level):
+            out = dot(three_planes(deltas.at[level], first, count), wide, NT if level == 0 else NN)
+            rows = count * 64
+            back = (
+                pltpu.roll(out[:, :128], rows - 1, 0)
+                + out[:, 128:256]
+                + pltpu.roll(out[:, 256:], 1, 0)
+            ).reshape(count, 64, 128)
+            if level > 0:
+                slope = slopes[level - 1, first : first + count]
+                deltas[level - 1, first : first + count] = (back * slope).astype(BF16)
+            else:
+                back_core[first - 8 : first - 8 + count] = back[:, 8:48]
         sum_scatter(level)
-        if level + 2 < 5:
-            sum_spread(level + 2)
-        if level + 1 < 5:
-            sum_across(level + 1)
-        taps = taps_ref[level]
-        wide = [
-            jnp.concatenate([taps[3 * k], taps[3 * k + 1], taps[3 * k + 2]], axis=1)
-            for k in (2, 1, 0)
-        ]
-        spread_out = dot(deltas[level, 1], wide[1])
-        halo_wait(deltas, 5, level)
-        sides = jnp.concatenate([deltas[level, 0], deltas[level, 2]], axis=1)
-        spread_out += dot(sides, jnp.concatenate([wide[0], wide[2]], axis=0))
-        back = (
-            shifted(spread_out[:, :128], -1)
-            + spread_out[:, 128:256]
-            + shifted(spread_out[:, 256:], 1)
-        )
-        if level > 0:
-            pre = pres[level - 1]
-            sigmoid = jax.nn.sigmoid(pre)
-            rounded = (back * (sigmoid * (1.0 + pre * (1.0 - sigmoid)))).astype(BF16)
-            deltas[level - 1, 1] = rounded
-            halo_start(deltas, 5, level - 1)
-            delta = rounded.astype(F32)
-        else:
-            grad_ref[...] = direct[...] + back
+        if level == 0:
+            sum_across(4)
+
+    @pl.loop(1, 8)
+    def _(turn):
+        other = lax.rem(y_block + turn, 8)
+        pltpu.make_async_remote_copy(
+            back_core.at[other], back_rows.at[y_block],
+            block_send.at[2, 0], block_recv.at[2, 0], (subj, z_block * 8 + other), MESH,
+        ).start()
+
+    back_rows[y_block] = back_core[y_block]
+    sum_across(3)
+    sum_across(2)
+    sum_across(1)
+    sum_spread(4)
     sum_across(0)
-    sum_spread(1)
-    sum_spread(0)
+    for level in (3, 2, 1, 0):
+        sum_spread(level)
+    bulk_wait(back_core, 7, block_send.at[2, 0])
+    bulk_wait(back_rows, 7, block_recv.at[2, 0])
+    grad_ref[...] = direct[...] + back_rows[...].reshape(NY, 128)
+    for level in (4, 3, 2, 1, 0):
+        sum_share(level)
     for level in (4, 3, 2, 1, 0):
         sum_finish(level)
 
 
-def main_call(u, s, up, image, taps, kt):
+def main_call(u, s, up, image, weights, kt):
     eu, es, eo, rows, rows_back, depth, depth_back, spread = tables()
     vmem = pl.BlockSpec(memory_space=pltpu.VMEM)
     hbm = pl.BlockSpec(memory_space=pl.ANY)
@@ -509,10 +587,11 @@
             jax.ShapeDtypeStruct((3, 1024, 128), BF16),
             jax.ShapeDtypeStruct((2, 512, 128), BF16),
         ),
-        in_specs=[vmem] * 9 + [hbm] * 5,
+        in_specs=[vmem] * 13 + [hbm] * 5,
         out_specs=(vmem, vmem, vmem),
         scratch_shapes=[pltpu.VMEM(t.shape, BF16) for t in big]
         + [
+            pltpu.VMEM((5, 9, 128, 128), BF16),
             pltpu.VMEM((256, 768), BF16),
             pltpu.VMEM((NY, 512), F32),
             pltpu.VMEM((SLABS, 16, 128), BF16),
@@ -523,13 +602,24 @@
             pltpu.VMEM((1024, 256), BF16),
             pltpu.VMEM((19, 448, 128), F32),
             pltpu.VMEM((NY, 128), F32),
-            pltpu.VMEM((5, 3, NY, 128), BF16),
-            pltpu.VMEM((4, NY, 128), F32),
-            pltpu.VMEM((5, 3, NY, 128), BF16),
+            pltpu.VMEM((NY + 24, 128), F32),
+            pltpu.VMEM((8, 64, 128), BF16),
+            pltpu.VMEM((8, 64, 128), BF16),
+            pltpu.VMEM((5, 24, 64, 128), BF16),
+            pltpu.VMEM((4, 24, 64, 128), F32),
+            pltpu.VMEM((5, 24, 64, 128), BF16),
+            pltpu.VMEM((24, 64, 128), F32),
+            pltpu.VMEM((8, 40, 128), F32),
+            pltpu.VMEM((8, 40, 128), F32),
             pltpu.VMEM((3, 32, 32, 128), BF16),
             pltpu.VMEM((2, 32, 16, 128), BF16),
-            pltpu.VMEM((3, 32, 32, 128), BF16),
-            pltpu.VMEM((2, 32, 16, 128), BF16),
+        ]
+        + [
+            pltpu.VMEM(shape, BF16)
+            for _ in range(3)
+            for shape in ((3, 16, 32, 128), (2, 16, 16, 128))
+        ]
+        + [
             pltpu.VMEM((3, 1, 32, 128), BF16),
             pltpu.VMEM((2, 1, 16, 128), BF16),
             pltpu.VMEM((3, 8, 32, 128), BF16),
@@ -539,10 +629,10 @@
             pltpu.SemaphoreType.DMA((5,)),
             pltpu.SemaphoreType.DMA((2,)),
             pltpu.SemaphoreType.DMA((2,)),
-            pltpu.SemaphoreType.DMA((10, 2)),
-            pltpu.SemaphoreType.DMA((10, 2)),
-            pltpu.SemaphoreType.DMA((5, 3)),
-            pltpu.SemaphoreType.DMA((5, 3)),
+            pltpu.SemaphoreType.DMA((3, 3)),
+            pltpu.SemaphoreType.DMA((3, 3)),
+            pltpu.SemaphoreType.DMA((5, 5)),
+            pltpu.SemaphoreType.DMA((5, 5)),
         ],
         compiler_params=pltpu.CompilerParams(
             collective_id=0, has_side_effects=True, vmem_limit_bytes=50 * 1024 * 1024
@@ -551,7 +641,7 @@
             flops=8_000_000_000, bytes_accessed=20_000_000, transcendentals=400_000
         ),
         name="step",
-    )(u, s, up, image, taps, kt, eu, es, eo, rows, rows_back, depth, depth_back, spread)
+    )(u, s, up, image, *weights, kt, eu, es, eo, rows, rows_back, depth, depth_back, spread)
 
 
 def finish_kernel(scale, mid_ref, small_ref, first_ref, second_ref, third_ref, fourth_ref, last_ref):
@@ -615,15 +705,16 @@
 
     up = cells_first(upstream[0, :, 0])
     image_cells = cells_first(image[0, :, 0])
-    first = jnp.pad(w_first, ((0, 0),) * 4 + ((0, 44),))
-    last = jnp.pad(w_last, ((0, 0),) * 3 + ((0, 44), (0, 0)))
-    every = jnp.stack([first, w_second, w_third, w_fourth, last])
-    top = jnp.concatenate([every[:, :, 1], every[:, :, 2]], axis=-1)
-    bottom = jnp.concatenate([every[:, :, 0], every[:, :, 1]], axis=-1)
-    taps = jnp.concatenate([top, bottom], axis=3).reshape(5, 9, 128, 128)
+    weights = (
+        jnp.swapaxes(w_first.reshape(27, 64, 20), 1, 2),
+        w_second.reshape(27, 64, 64),
+        w_third.reshape(27, 64, 64),
+        w_fourth.reshape(27, 64, 64),
+        w_last.reshape(27, 20, 64),
+    )
     kt = jnp.transpose(kernel, (4, 3, 2, 0, 1)).astype(BF16).reshape(10, NZ, 100)
     kt = jnp.pad(kt, ((0, 0), (0, 0), (0, 28)))
-    grad, mid, small = main_call(u, s, up, image_cells, taps, kt)
+    grad, mid, small = main_call(u, s, up, image_cells, weights, kt)
     cells = (
         lax.axis_size("subj") * image.shape[0] * lax.axis_size("slab") * image.shape[2] * 2 * NY
     )

time: 105 us -> 86.5 us (0.82)
  Pallas kernels: 97.1 us -> 78.2 us
    pallas_call x1, Pallas kernels: 95.2 us -> 76.3 us  [main_call(): pl.pallas_call(main_kernel, out_shape=(jax.ShapeDtypeStruct((NY, 128), F3...]
    concatenate x1 -> x0, other arithmetic: 1.93 us -> none  [body(): taps = jnp.concatenate([top, bottom], axis=3).reshape(5, 9, 128, 128)]
    unnamed x30 -> x19, local copies, waits for them, and re-layouts: 3.54 us -> 3.21 us
where the time goes in v2:
time: 86.5 us; the launch traced here: 86.2 us
  Pallas kernels  78.2 us (90%)
  local copies, waits for them, and re-layouts  4.13 us (5%)
  other arithmetic  3.01 us (3%)
    pallas_call x1, Pallas kernels, main_call(): pl.pallas_call(main_kernel, out_shape=(jax.ShapeDtypeStruct((NY, 128), F3...  76.3 us
    unnamed x19, local copies, waits for them, and re-layouts  3.21 us
    pallas_call x1, Pallas kernels, finish_call(): pl.pallas_call(functools.partial(finish_kernel, 1.0 / math.sqrt(cells)),...  1.93 us

profile of v2, /device:TPU:1, one launch (start us, length us, event | category | flops | bytes accessed | tf_op | source)
XLA Modules:
  0.0 86.2 jit_solution(14423691679145760834)
XLA Ops:
  0.6 0.8 convert_element_type.24
  1.5 0.0 copy-start
  1.5 0.0 copy-start.1
  1.5 0.0 copy-start.2
  1.5 0.0 copy-start.3
  1.5 0.0 copy-start.4
  1.5 0.0 copy-start.5
  1.5 0.0 copy-start.6
  1.6 1.0 %convert_element_type.22 = bf16[1,20,1,2,320]{4,3,2,1,0:T(2,128)(2,1)S(1)} convert(f32[1,20,1,2,320]{4,3,2,1,0:T(2,128)} %param.18) | non-fusion elementwise | flops 12800 | bytes 76800 | tf_op jit(solution)/shard_map/convert_element_type | solution.py:699
  2.6 0.8 copy.38
  3.4 0.1 copy.32.image_ref
  3.5 0.8 copy.37
  4.3 0.1 copy.31.up_ref
  4.5 1.2 %convert_bitcast_fusion = bf16[5,2,64,10,10]{2,1,0,4,3:T(2,128)(2,1)S(1)} fusion(f32[10,10,64,2,5]{2,3,4,1,0:T(2,128)} %param.20), kind=kLoop, calls=%fused_computation | loop fusion | flops 64000 | bytes 384000 | tf_op jit(solution)/shard_map/convert_element_type | solution.py:715
  5.7 0.1 reshape.70
  5.8 0.3 copy.30
  6.2 0.0 copy-done
  6.2 0.0 copy-done.1
  6.2 0.0 copy-done.2
  6.2 0.0 copy-done.3
  6.2 0.0 copy-done.4
  6.2 0.0 copy-done.5
  6.2 0.0 copy-done.6
  6.2 0.0 copy-start.7
  6.2 0.9 %copy-done.7 = bf16[512,40]{1,0:T(8,128)(2,1)S(1)} copy-done((bf16[512,40]{1,0:T(8,128)(2,1)S(1)}, bf16[512,40]{1,0:T(8,128)(2,1)}, u32[]{:S(2)}) %copy-start.7) | copy-done | bytes 40984
  7.1 76.3 %step.1 = (f32[320,128]{1,0:T(8,128)S(1)}, bf16[3,1024,128]{2,1,0:T(8,128)(2,1)S(1)}, bf16[2,512,128]{2,1,0:T(8,128)(2,1)S(1)}) custom-call(bf16[40,320]{1,0:T(8,128)(2,1)S(1)} %convert_element_type.23.u_ref, bf16[32,320]{1,0:T(8,128)(2,1)S(1)} %convert_element_type.25.s_ref, f32[320,128]{1,0:T(8,128)S(1)} %copy.31.up_ref, ...), custom_call_target="tpu_custom_call" | custom-call | flops 8000000000 | bytes 20000000 | tf_op jit(solution)/shard_map/step/pallas_call | solution.py:583
  83.4 0.1 copy.33
  83.6 0.7 copy.34
  84.2 1.9 %finish.1 = (f32[27,20,64]{2,1,0:T(8,128)}, f32[27,64,64]{2,1,0:T(8,128)}, f32[27,64,64]{2,1,0:T(8,128)}, f32[27,64,64]{2,1,0:T(8,128)}, f32[27,20,64]{2,1,0:T(8,128)}) custom-call(bf16[3,1024,128]{2,1,0:T(8,128)(2,1)S(1)} %get-tuple-element.15.mid_ref, bf16[2,512,128]{2,1,0:T(8,128)(2,1)S(1)} %get-tuple-element.16.small_ref), custom_call_target="tpu_custom_call" | custom-call | tf_op jit(solution)/shard_map/finish/pallas_call | solution.py:688
  (6 shorter events, 0.1 us)
Async XLA Ops:
  1.5 4.7 %copy-start = (bf16[3,3,3,64,64]{4,3,2,1,0:T(8,128)(2,1)S(1)}, bf16[3,3,3,64,64]{4,3,2,1,0:T(8,128)(2,1)}, u32[]{:S(2)}) copy-start(bf16[3,3,3,64,64]{4,3,2,1,0:T(8,128)(2,1)} %param.22) | copy-start | bytes 663556
  1.5 4.7 %copy-start.1 = (bf16[3,3,3,64,64]{4,3,2,1,0:T(8,128)(2,1)S(1)}, bf16[3,3,3,64,64]{4,3,2,1,0:T(8,128)(2,1)}, u32[]{:S(2)}) copy-start(bf16[3,3,3,64,64]{4,3,2,1,0:T(8,128)(2,1)} %param.23) | copy-start | bytes 663556
  1.5 4.7 %copy-start.2 = (bf16[3,3,3,64,64]{4,3,2,1,0:T(8,128)(2,1)S(1)}, bf16[3,3,3,64,64]{4,3,2,1,0:T(8,128)(2,1)}, u32[]{:S(2)}) copy-start(bf16[3,3,3,64,64]{4,3,2,1,0:T(8,128)(2,1)} %param.24) | copy-start | bytes 663556
  1.5 4.7 %copy-start.3 = (bf16[3,3,3,64,20]{3,4,2,1,0:T(8,128)(2,1)S(1)}, bf16[3,3,3,64,20]{3,4,2,1,0:T(8,128)(2,1)}, u32[]{:S(2)}) copy-start(bf16[3,3,3,64,20]{3,4,2,1,0:T(8,128)(2,1)} %param.21) | copy-start | bytes 207364
  1.5 4.7 %copy-start.4 = (bf16[3,3,3,20,64]{4,3,2,1,0:T(8,128)(2,1)S(1)}, bf16[3,3,3,20,64]{4,3,2,1,0:T(8,128)(2,1)}, u32[]{:S(2)}) copy-start(bf16[3,3,3,20,64]{4,3,2,1,0:T(8,128)(2,1)} %param.25) | copy-start | bytes 207364
  1.5 4.7 %copy-start.5 = (bf16[512,128]{1,0:T(8,128)(2,1)S(1)}, bf16[512,128]{1,0:T(8,128)(2,1)}, u32[]{:S(2)}) copy-start(bf16[512,128]{1,0:T(8,128)(2,1)} %constant.23.clone.eo_ref) | copy-start | bytes 393220
  1.5 4.7 %copy-start.6 = (bf16[512,32]{1,0:T(8,128)(2,1)S(1)}, bf16[512,32]{1,0:T(8,128)(2,1)}, u32[]{:S(2)}) copy-start(bf16[512,32]{1,0:T(8,128)(2,1)} %constant.22.clone.es_ref) | copy-start | bytes 98308
  6.2 0.9 %copy-start.7 = (bf16[512,40]{1,0:T(8,128)(2,1)S(1)}, bf16[512,40]{1,0:T(8,128)(2,1)}, u32[]{:S(2)}) copy-start(bf16[512,40]{1,0:T(8,128)(2,1)} %constant.21.clone.eu_ref) | copy-start | bytes 122884

commit v3 on v2

--- a/solution.py
+++ b/solution.py
@@ -39,16 +39,16 @@
 @functools.lru_cache(None)
 def tables():
     half = ml_dtypes.bfloat16
-    expand_u = np.zeros((512, 40), np.float32)
-    expand_s = np.zeros((512, 32), np.float32)
+    expand_u = np.zeros((2, 512, 20), np.float32)
+    expand_s = np.zeros((2, 512, 16), np.float32)
     collect = np.zeros((512, 128), np.float32)
     for x in range(2):
         for comp in range(10):
             for coil in range(8):
                 lane = lane_of(x, comp, coil)
                 for part in range(2):
-                    expand_u[part * 256 + lane, (part * 10 + comp) * 2 + x] = 1
-                    expand_s[part * 256 + lane, part * 16 + coil * 2 + x] = 1
+                    expand_u[x, part * 256 + lane, part * 10 + comp] = 1
+                    expand_s[x, part * 256 + lane, part * 8 + coil] = 1
                     collect[part * 256 + lane, x * 64 + part * 10 + comp] = 1
     y = np.arange(NY)
     angle = 2 * np.pi * ((y[:, None] * y[None, :]) % NY) / NY
@@ -100,18 +100,22 @@
     return lax.dot_general(a, b, dims, preferred_element_type=F32)
 
 
-def main_kernel(
-    u_ref, s_ref, up_ref, image_ref, w1_ref, w2_ref, w3_ref, w4_ref, w5_ref, kt_ref,
-    eu_ref, es_ref, eo_ref,
-    rows_hbm, rows_back_hbm, depth_hbm, depth_back_hbm, spread_hbm,
-    grad_ref, sums_mid_ref, sums_small_ref,
-    rows_t, rows_back_t, depth_t, depth_back_t, spread_t,
-    taps_ref, coil, maps, message, arrived, mixed, message_back, returned, unpacked, coefs, direct,
-    padded, stage_image, stage_delta, acts, slopes, deltas, inside, back_core, back_rows, parts_mid, parts_small, halves_mid, halves_small,
-    folded_mid, folded_small, gathered_mid, gathered_small,
-    own_mid, own_small, across_mid, across_small, total_mid, total_small,
-    table_sem, send_sem, recv_sem, block_send, block_recv, sum_send, sum_recv,
-):
+def main_kernel(*refs):
+    sources, refs = refs[:17], refs[17:]
+    grad_ref, sums_mid_ref, sums_small_ref = refs[:3]
+    held, refs = refs[3:20], refs[20:]
+    (
+        up_ref, s_ref, eu_ref, es_ref, rows_t, image_ref, w1_ref, w2_ref, w3_ref, w4_ref, w5_ref,
+        k_ref, spread_t, depth_t, depth_back_t, eo_ref, rows_back_t,
+    ) = held
+    (
+        taps_ref, coil, maps, message, arrived, mixed, message_back, returned, unpacked, coefs,
+        direct, up_rows, padded, stage_image, stage_delta, packed_image, packed_delta, acts, slopes,
+        deltas, inside, back_core, back_rows, parts_mid, parts_small, halves_mid, halves_small,
+        folded_mid, folded_small, gathered_mid, gathered_small, own_mid, own_small, across_mid,
+        across_small, total_mid, total_small, table_sem, send_sem, recv_sem, block_send, block_recv,
+        sum_send, sum_recv,
+    ) = refs
     subj = lax.axis_index("subj")
     slab = lax.axis_index("slab")
     z_hi, core = subj // 2, subj % 2
@@ -133,13 +137,13 @@
         return other, ((other // 4) * 2 + core, (other % 4) * 16 + place)
 
     z_block, y_block = slab // 8, slab % 8
-    zero_planes = jnp.zeros((8, 64, 128), BF16)
+    zero_planes = jnp.zeros((8, 32, 128), BF16)
     for first, edge in ((0, 0), (16, 7)):
 
         @pl.when(z_block == edge)
         def _(first=first):
-            acts[0, first : first + 8] = zero_planes
-            deltas[4, first : first + 8] = zero_planes
+            packed_image[first : first + 8] = zero_planes
+            packed_delta[first : first + 8] = zero_planes
 
     barrier = pltpu.get_barrier_semaphore()
 
@@ -158,17 +162,10 @@
 
     fetches = [
         pltpu.make_async_copy(source, target, table_sem.at[i])
-        for i, (source, target) in enumerate(
-            (
-                (rows_hbm, rows_t),
-                (spread_hbm, spread_t),
-                (depth_hbm, depth_t),
-                (depth_back_hbm, depth_back_t),
-                (rows_back_hbm, rows_back_t),
-            )
-        )
+        for i, (source, target) in enumerate(zip(sources, held))
     ]
-    fetches[0].start()
+    for fetch in fetches[:12]:
+        fetch.start()
 
     for i in range(3):
         parts_mid[i, 28:32] = jnp.zeros((4, 32, 128), BF16)
@@ -177,11 +174,18 @@
     def cut(block, stage):
         padded[8 : 8 + NY, :] = block
         for piece in range(8):
-            stage[piece] = padded[40 * piece : 40 * piece + 64, :].astype(BF16)
+            upper = padded[40 * piece : 40 * piece + 32, :]
+            lower = padded[40 * piece + 32 : 40 * piece + 64, :]
+            stage[piece] = (upper + pltpu.roll(lower, 32, 1)).astype(BF16)
+
+    def unpack(source, target):
+        block = source[...]
+        lower = pltpu.roll(block.astype(F32).reshape(24 * 32, 128), 96, 1).astype(BF16)
+        target[:, 0:32] = block
+        target[:, 32:64] = lower.reshape(24, 32, 128)
 
     padded[0:8, :] = jnp.zeros((8, 128), F32)
     padded[8 + NY :, :] = jnp.zeros((16, 128), F32)
-    cut(image_ref[...].astype(F32), stage_image)
 
     def blocks_send(stage, target, which):
         for group, step in ((1, -1), (2, 1), (0, 0)):
@@ -234,17 +238,21 @@
         bulk_wait(source, SLABS - 1, send_sem.at[which])
         bulk_wait(target, SLABS - 1, recv_sem.at[which])
 
-    wide_u = dot(eu_ref[...], u_ref[...])
-    wide_s = dot(es_ref[...], s_ref[...])
+    for fetch in fetches[:4]:
+        fetch.wait()
+    lane = lax.broadcasted_iota(jnp.int32, (20, 128), 1)
+    channel = lax.broadcasted_iota(jnp.int32, (20, 128), 0)
+    places = [jnp.where(lane == x * 64 + channel, 1.0, 0.0).astype(BF16) for x in range(2)]
+    u_high = [up_ref[:, x, :].astype(BF16) for x in range(2)]
+    s_high = [s_ref[:, x, :].astype(BF16) for x in range(2)]
+    wide_u = dot(eu_ref[0], u_high[0]) + dot(eu_ref[1], u_high[1])
+    wide_s = dot(es_ref[0], s_high[0]) + dot(es_ref[1], s_high[1])
     u_re, u_im = wide_u[:256], wide_u[256:]
     s_re, s_im = wide_s[:256], wide_s[256:]
     coil[...] = jnp.zeros((256, 768), BF16)
     coil[:, 0:NY] = (s_re * u_re - s_im * u_im).astype(BF16)
     coil[:, 384 : 384 + NY] = (s_re * u_im + s_im * u_re).astype(BF16)
-    maps[...] = dot(s_ref[...], es_ref[...], (((0,), (1,)), ((), ())))
-    fetches[0].wait()
-    for fetch in fetches[1:]:
-        fetch.start()
+    fetches[4].wait()
     sub = lax.broadcasted_iota(jnp.int32, (8, 8, 128), 1) // 2
 
     @pl.loop(0, 8)
@@ -299,6 +307,22 @@
             acts[level + 1, first : first + count] = value.astype(BF16).reshape(count, 64, 128)
             slopes[level, first : first + count] = slope.reshape(count, 64, 128)
 
+    for fetch in fetches[12:]:
+        fetch.start()
+    fetches[5].wait()
+    image = image_ref[...].astype(F32)
+    cut(
+        sum(dot(image[:, x, :].astype(BF16), places[x], TN) for x in range(2)), stage_image
+    )
+    crossed = (((0,), (1,)), ((), ()))
+    maps[...] = dot(s_high[0], es_ref[0], crossed) + dot(s_high[1], es_ref[1], crossed)
+    rows_sum = jnp.zeros((NY, 128), F32)
+    for x in range(2):
+        low = (up_ref[:, x, :] - u_high[x].astype(F32)).astype(BF16)
+        rows_sum += dot(u_high[x], places[x], TN) + dot(low, places[x], TN)
+    up_rows[...] = rows_sum
+    for fetch in fetches[6:12]:
+        fetch.wait()
     for level, w_ref in enumerate((w1_ref, w2_ref, w3_ref, w4_ref, w5_ref)):
         for tap in range(9):
             low, middle, high = [
@@ -315,35 +339,34 @@
 
     pl.semaphore_wait(barrier, 68)
     exchange_start(message, arrived, 0)
-    blocks_send(stage_image, acts.at[0], 0)
-    fetches[1].wait()
-    blocks = []
+    blocks_send(stage_image, packed_image, 0)
+    fetches[12].wait()
+    columns = []
     for q in range(7):
-        picks = [slot_block(q, j) for j in range(3)]
-        blocks.append(jnp.concatenate([kt_ref[ky * 2 + x] for ky, x in picks], axis=1))
-    stacked = jnp.concatenate(blocks, axis=0)
+        rows = []
+        for j in range(3):
+            ky, x = slot_block(q, j)
+            rows += [k_ref[:, ky, x, :], jnp.zeros((28, NZ), F32)]
+        columns.append(jnp.concatenate(rows, axis=0))
+    stacked = jnp.concatenate(columns, axis=1).astype(BF16)
     for step in range(10):
-        pair = dot(stacked, spread_t[:, step * 256 : step * 256 + 256])
+        pair = dot(stacked, spread_t[:, step * 256 : step * 256 + 256], TN)
         coefs[2 * step] = pair[:, :128]
         if step < 9:
             coefs[2 * step + 1] = pair[:, 128:]
-    blocks_wait(stage_image, acts.at[0], 0)
-    forward(0)
-    forward(1)
-
-    fetches[2].wait()
-    fetches[3].wait()
+
+    fetches[13].wait()
+    fetches[14].wait()
     exchange_wait(message, arrived, 0)
 
-    @pl.loop(0, 7)
-    def _(q):
-        first = pl.multiple_of(q * 128, 128)
+    for q in range(7):
+        first = q * 128
         spectrum = dot(depth_t[pl.ds(first, 128), :], arrived[...].reshape(1024, 128))
         real, imag = spectrum[:64], spectrum[64:]
         out_real = jnp.zeros((64, 128), F32)
         out_imag = jnp.zeros((64, 128), F32)
         for shift in range(-9, 10):
-            factor = coefs[shift + 9, pl.ds(pl.multiple_of(q * 64, 64), 64), :]
+            factor = coefs[shift + 9, q * 64 : q * 64 + 64, :]
             turn = (-4 * shift) % 128
             moved_real = real if turn == 0 else pltpu.roll(real, turn, 1)
             moved_imag = imag if turn == 0 else pltpu.roll(imag, turn, 1)
@@ -352,15 +375,16 @@
         mixed[pl.ds(first, 64), :] = out_real.astype(BF16)
         mixed[pl.ds(first + 64, 64), :] = out_imag.astype(BF16)
 
-    @pl.loop(0, 8)
-    def _(step):
-        first = pl.multiple_of(step * 128, 128)
-        back = dot(depth_back_t[pl.ds(first, 128), :], mixed[...])
-        message_back[pl.ds(step * 8, 8)] = back.astype(BF16).reshape(8, 16, 128)
+    for step in range(2):
+        first = step * 512
+        back = dot(depth_back_t[pl.ds(first, 512), :], mixed[...])
+        message_back[pl.ds(step * 32, 32)] = back.astype(BF16).reshape(32, 16, 128)
 
     exchange_start(message_back, returned, 1)
-    forward(2)
-    forward(3)
+    blocks_wait(stage_image, packed_image, 0)
+    unpack(packed_image, acts.at[0])
+    for level in range(4):
+        forward(level)
     exchange_wait(message_back, returned, 1)
 
     @pl.loop(0, 8)
@@ -383,17 +407,18 @@
         unpacked[pl.ds(first, 128), 0:128] = block.reshape(128, 128).astype(BF16)
         unpacked[pl.ds(first, 128), 128:256] = rest.astype(BF16)
 
-    fetches[4].wait()
+    fetches[15].wait()
+    fetches[16].wait()
     back_re = dot(rows_back_t[0:NY, :], unpacked[...])
     back_im = dot(rows_back_t[NY:, :], unpacked[...])
     s_re, s_im = maps[:, :256], maps[:, 256:]
     out_re = (s_re * back_re + s_im * back_im).astype(BF16)
     out_im = (s_re * back_im - s_im * back_re).astype(BF16)
     normal = dot(out_re, eo_ref[0:256, :]) + dot(out_im, eo_ref[256:, :])
-    own_direct = up_ref[...] - 0.5 * normal
+    own_direct = up_rows[...] - 0.5 * normal
     direct[...] = own_direct
     cut(own_direct, stage_delta)
-    blocks_send(stage_delta, deltas.at[4], 1)
+    blocks_send(stage_delta, packed_delta, 1)
 
     def buffers_of(level):
         if level in (0, 4):
@@ -518,7 +543,8 @@
                 both = jnp.concatenate([slots[2 * k], slots[2 * k + 1]], axis=0)
                 parts[3 * k : 3 * k + 3] = both.astype(BF16).reshape(3, 16, 128)
 
-    blocks_wait(stage_delta, deltas.at[4], 1)
+    blocks_wait(stage_delta, packed_delta, 1)
+    unpack(packed_delta, deltas.at[4])
     for level in (4, 3, 2, 1, 0):
         weight_part(level)
         sum_halves(level)
@@ -575,11 +601,12 @@
         sum_finish(level)
 
 
-def main_call(u, s, up, image, weights, kt):
+def main_call(up, s, image, weights, kernel):
     eu, es, eo, rows, rows_back, depth, depth_back, spread = tables()
     vmem = pl.BlockSpec(memory_space=pltpu.VMEM)
-    hbm = pl.BlockSpec(memory_space=pl.ANY)
-    big = [rows, rows_back, depth, depth_back, spread]
+    sources = [
+        up, s, eu, es, rows, image, *weights, kernel, spread, depth, depth_back, eo, rows_back
+    ]
     return pl.pallas_call(
         main_kernel,
         out_shape=(
@@ -587,9 +614,9 @@
             jax.ShapeDtypeStruct((3, 1024, 128), BF16),
             jax.ShapeDtypeStruct((2, 512, 128), BF16),
         ),
-        in_specs=[vmem] * 13 + [hbm] * 5,
+        in_specs=[pl.BlockSpec(memory_space=pl.ANY)] * len(sources),
         out_specs=(vmem, vmem, vmem),
-        scratch_shapes=[pltpu.VMEM(t.shape, BF16) for t in big]
+        scratch_shapes=[pltpu.VMEM(t.shape, t.dtype) for t in sources]
         + [
             pltpu.VMEM((5, 9, 128, 128), BF16),
             pltpu.VMEM((256, 768), BF16),
@@ -602,9 +629,12 @@
             pltpu.VMEM((1024, 256), BF16),
             pltpu.VMEM((19, 448, 128), F32),
             pltpu.VMEM((NY, 128), F32),
+            pltpu.VMEM((NY, 128), F32),
             pltpu.VMEM((NY + 24, 128), F32),
-            pltpu.VMEM((8, 64, 128), BF16),
-            pltpu.VMEM((8, 64, 128), BF16),
+            pltpu.VMEM((8, 32, 128), BF16),
+            pltpu.VMEM((8, 32, 128), BF16),
+            pltpu.VMEM((24, 32, 128), BF16),
+            pltpu.VMEM((24, 32, 128), BF16),
             pltpu.VMEM((5, 24, 64, 128), BF16),
             pltpu.VMEM((4, 24, 64, 128), F32),
             pltpu.VMEM((5, 24, 64, 128), BF16),
@@ -626,7 +656,7 @@
             pltpu.VMEM((2, 8, 16, 128), BF16),
             pltpu.VMEM((3, 32, 32, 128), BF16),
             pltpu.VMEM((2, 32, 16, 128), BF16),
-            pltpu.SemaphoreType.DMA((5,)),
+            pltpu.SemaphoreType.DMA((17,)),
             pltpu.SemaphoreType.DMA((2,)),
             pltpu.SemaphoreType.DMA((2,)),
             pltpu.SemaphoreType.DMA((3, 3)),
@@ -635,13 +665,13 @@
             pltpu.SemaphoreType.DMA((5, 5)),
         ],
         compiler_params=pltpu.CompilerParams(
-            collective_id=0, has_side_effects=True, vmem_limit_bytes=50 * 1024 * 1024
+            collective_id=0, has_side_effects=True, vmem_limit_bytes=60 * 1024 * 1024
         ),
         cost_estimate=pl.CostEstimate(
             flops=8_000_000_000, bytes_accessed=20_000_000, transcendentals=400_000
         ),
         name="step",
-    )(u, s, up, image, *weights, kt, eu, es, eo, rows, rows_back, depth, depth_back, spread)
+    )(*sources)
 
 
 def finish_kernel(scale, mid_ref, small_ref, first_ref, second_ref, third_ref, fourth_ref, last_ref):
@@ -696,15 +726,6 @@
 
 
 def body(image, upstream, coil_maps, kernel, w_first, w_second, w_third, w_fourth, w_last):
-    u = upstream[0].reshape(40, NY).astype(BF16)
-    s = coil_maps[0].reshape(32, NY).astype(BF16)
-
-    def cells_first(block):
-        turned = jnp.transpose(block, (2, 1, 0))
-        return jnp.pad(turned, ((0, 0), (0, 0), (0, 44))).reshape(NY, 128)
-
-    up = cells_first(upstream[0, :, 0])
-    image_cells = cells_first(image[0, :, 0])
     weights = (
         jnp.swapaxes(w_first.reshape(27, 64, 20), 1, 2),
         w_second.reshape(27, 64, 64),
@@ -712,9 +733,10 @@
         w_fourth.reshape(27, 64, 64),
         w_last.reshape(27, 20, 64),
     )
-    kt = jnp.transpose(kernel, (4, 3, 2, 0, 1)).astype(BF16).reshape(10, NZ, 100)
-    kt = jnp.pad(kt, ((0, 0), (0, 0), (0, 28)))
-    grad, mid, small = main_call(u, s, up, image_cells, weights, kt)
+    bands = jnp.transpose(kernel, (0, 1, 4, 3, 2)).reshape(100, 5, 2, NZ)
+    grad, mid, small = main_call(
+        upstream[0, :, 0], coil_maps[0].reshape(16, 2, NY), image[0, :, 0], weights, bands
+    )
     cells = (
         lax.axis_size("subj") * image.shape[0] * lax.axis_size("slab") * image.shape[2] * 2 * NY
     )

time: 86.5 us -> 75.6 us (0.87)
  Pallas kernels: 78.2 us -> 71 us
  other arithmetic: 3.01 us -> 0 us
    pallas_call x1, Pallas kernels: 76.3 us -> 69 us  [main_call(): pl.pallas_call(main_kernel, out_shape=(jax.ShapeDtypeStruct((NY, 128), F3...]
    convert_element_type x3 -> x0, other arithmetic: 3.01 us -> none  [the longest x1 1.22 us: body(): jnp.transpose(kernel, (4, 3, 2, 0, 1)).astype(BF16).reshape(10, NZ, 100)]
    pallas_call x1, local copies, waits for them, and re-layouts: 0.13 us -> 1.04 us  [main_call(): pl.pallas_call(main_kernel, out_shape=(jax.ShapeDtypeStruct((NY, 128), F3...]
    unnamed x19 -> x5, local copies, waits for them, and re-layouts: 3.21 us -> 2.74 us
where the time goes in v3:
time: 75.6 us; the launch traced here: 75.4 us
  Pallas kernels  71 us (94%)
  local copies, waits for them, and re-layouts  3.79 us (5%)
    pallas_call x1, Pallas kernels, main_call(): pl.pallas_call(main_kernel, out_shape=(jax.ShapeDtypeStruct((NY, 128), F3...  69 us
    unnamed x5, local copies, waits for them, and re-layouts  2.74 us
    pallas_call x1, Pallas kernels, finish_call(): pl.pallas_call(functools.partial(finish_kernel, 1.0 / math.sqrt(cells)),...  1.93 us

profile of v3, /device:TPU:1, one launch (start us, length us, event | category | flops | bytes accessed | tf_op | source)
XLA Modules:
  0.0 75.4 jit_solution(4417570965547819443)
XLA Ops:
  0.6 69.0 %step.1 = (f32[320,128]{1,0:T(8,128)}, bf16[3,1024,128]{2,1,0:T(8,128)(2,1)}, bf16[2,512,128]{2,1,0:T(8,128)(2,1)}) custom-call(f32[20,2,320]{2,1,0:T(2,128)} %bitcast.37, f32[16,2,320]{2,1,0:T(2,128)} %bitcast.38, bf16[2,512,20]{2,1,0:T(8,128)(2,1)} %constant.16.clone.refs_2_, bf16[2,512,16]{2,1,0:T(8,128)(2,1)} %constant.17.clone.refs_3_, ...), custom_call_target="tpu_custom_call" | custom-call | flops 8000000000 | bytes 20000000 | tf_op jit(solution)/shard_map/step/pallas_call | solution.py:610
  69.7 1.0 %copy.24 = f32[320,128]{0,1:T(8,128)S(1)} copy(f32[320,128]{1,0:T(8,128)} %get-tuple-element.14) | data formatting | bytes 327680 | tf_op jit(solution)/shard_map/step/pallas_call | solution.py:610
  70.7 0.7 copy.25
  71.4 0.0 copy-start
  71.4 1.1 %copy-done = bf16[3,1024,128]{2,1,0:T(8,128)(2,1)S(1)} copy-done((bf16[3,1024,128]{2,1,0:T(8,128)(2,1)S(1)}, bf16[3,1024,128]{2,1,0:T(8,128)(2,1)}, u32[]{:S(2)}) %copy-start) | copy-done | bytes 786456
  72.5 0.0 copy-start.1
  72.5 0.9 %copy-done.1 = bf16[2,512,128]{2,1,0:T(8,128)(2,1)S(1)} copy-done((bf16[2,512,128]{2,1,0:T(8,128)(2,1)S(1)}, bf16[2,512,128]{2,1,0:T(8,128)(2,1)}, u32[]{:S(2)}) %copy-start.1) | copy-done | bytes 262168
  73.5 1.9 %finish.1 = (f32[27,20,64]{2,1,0:T(8,128)}, f32[27,64,64]{2,1,0:T(8,128)}, f32[27,64,64]{2,1,0:T(8,128)}, f32[27,64,64]{2,1,0:T(8,128)}, f32[27,20,64]{2,1,0:T(8,128)}) custom-call(bf16[3,1024,128]{2,1,0:T(8,128)(2,1)S(1)} %copy-done, bf16[2,512,128]{2,1,0:T(8,128)(2,1)S(1)} %copy-done.1), custom_call_target="tpu_custom_call" | custom-call | tf_op jit(solution)/shard_map/finish/pallas_call | solution.py:718
  (1 shorter events, 0.0 us)
Async XLA Ops:
  71.4 1.1 %copy-start = (bf16[3,1024,128]{2,1,0:T(8,128)(2,1)S(1)}, bf16[3,1024,128]{2,1,0:T(8,128)(2,1)}, u32[]{:S(2)}) copy-start(bf16[3,1024,128]{2,1,0:T(8,128)(2,1)} %get-tuple-element.15.mid_ref) | copy-start | bytes 2359300
  72.5 0.9 %copy-start.1 = (bf16[2,512,128]{2,1,0:T(8,128)(2,1)S(1)}, bf16[2,512,128]{2,1,0:T(8,128)(2,1)}, u32[]{:S(2)}) copy-start(bf16[2,512,128]{2,1,0:T(8,128)(2,1)} %get-tuple-element.16.small_ref) | copy-start | bytes 786436

commit v4 on v3

--- a/solution.py
+++ b/solution.py
@@ -112,7 +112,7 @@
         taps_ref, coil, maps, message, arrived, mixed, message_back, returned, unpacked, coefs,
         direct, up_rows, padded, stage_image, stage_delta, packed_image, packed_delta, acts, slopes,
         deltas, inside, back_core, back_rows, parts_mid, parts_small, halves_mid, halves_small,
-        folded_mid, folded_small, gathered_mid, gathered_small, own_mid, own_small, across_mid,
+        folded_mid, folded_small, gathered_mid, gathered_small, gathered_first, own_mid, own_small, across_mid,
         across_small, total_mid, total_small, table_sem, send_sem, recv_sem, block_send, block_recv,
         sum_send, sum_recv,
     ) = refs
@@ -130,6 +130,10 @@
         other = lax.rem(place + step, 16)
         return other, (subj, z_lo * 16 + other)
 
+    def both_peer(step):
+        other = lax.rem(plane_index + step, 32)
+        return other, (z_hi * 2 + other // 16, z_lo * 16 + other % 16)
+
     twin = (z_hi * 2 + 1 - core, slab)
 
     def depth_peer(step):
@@ -154,7 +158,9 @@
     def _(step):
         greet(slab_peer(step))
 
-    greet(twin)
+    @pl.loop(0, 16)
+    def _(other):
+        greet((z_hi * 2 + 1 - core, z_lo * 16 + other))
 
     @pl.loop(0, 4)
     def _(other):
@@ -164,7 +170,7 @@
         pltpu.make_async_copy(source, target, table_sem.at[i])
         for i, (source, target) in enumerate(zip(sources, held))
     ]
-    for fetch in fetches[:12]:
+    for fetch in fetches[:5]:
         fetch.start()
 
     for i in range(3):
@@ -253,6 +259,8 @@
     coil[:, 0:NY] = (s_re * u_re - s_im * u_im).astype(BF16)
     coil[:, 384 : 384 + NY] = (s_re * u_im + s_im * u_re).astype(BF16)
     fetches[4].wait()
+    for fetch in fetches[5:]:
+        fetch.start()
     sub = lax.broadcasted_iota(jnp.int32, (8, 8, 128), 1) // 2
 
     @pl.loop(0, 8)
@@ -268,11 +276,6 @@
         extra = jnp.where(sub == 1, at_one, jnp.where(sub == 2, at_two, 0.0))
         packed = jnp.concatenate([body[:, 0:1], (body[:, 1] + extra)[:, None]], axis=1)
         message[pl.ds(step * 8, 8)] = packed.reshape(8, 16, 128).astype(BF16)
-
-    slot_z = lax.broadcasted_iota(jnp.int32, (24, 64, 128), 0) + (z_block * 8 - 8)
-    slot_y = lax.broadcasted_iota(jnp.int32, (24, 64, 128), 1) + (y_block * 40 - 8)
-    grid_ok = (slot_z >= 0) & (slot_z < NZ) & (slot_y >= 0) & (slot_y < NY)
-    inside[...] = jnp.where(grid_ok, 1.0, 0.0)
 
     def three_planes(buffer, first, count):
         pieces = [buffer[first + k : first + k + count].reshape(count * 64, 128) for k in (-1, 0, 1)]
@@ -307,13 +310,14 @@
             acts[level + 1, first : first + count] = value.astype(BF16).reshape(count, 64, 128)
             slopes[level, first : first + count] = slope.reshape(count, 64, 128)
 
-    for fetch in fetches[12:]:
-        fetch.start()
     fetches[5].wait()
     image = image_ref[...].astype(F32)
     cut(
         sum(dot(image[:, x, :].astype(BF16), places[x], TN) for x in range(2)), stage_image
     )
+    pl.semaphore_wait(barrier, 83)
+    exchange_start(message, arrived, 0)
+    blocks_send(stage_image, packed_image, 0)
     crossed = (((0,), (1,)), ((), ()))
     maps[...] = dot(s_high[0], es_ref[0], crossed) + dot(s_high[1], es_ref[1], crossed)
     rows_sum = jnp.zeros((NY, 128), F32)
@@ -337,9 +341,11 @@
                 ]
             taps_ref[level, tap] = jnp.concatenate(pieces, axis=0).astype(BF16)
 
-    pl.semaphore_wait(barrier, 68)
-    exchange_start(message, arrived, 0)
-    blocks_send(stage_image, packed_image, 0)
+    slot_z = lax.broadcasted_iota(jnp.int32, (24, 64, 128), 0) + (z_block * 8 - 8)
+    slot_y = lax.broadcasted_iota(jnp.int32, (24, 64, 128), 1) + (y_block * 40 - 8)
+    grid_ok = (slot_z >= 0) & (slot_z < NZ) & (slot_y >= 0) & (slot_y < NY)
+    inside[...] = jnp.where(grid_ok, 1.0, 0.0)
+
     fetches[12].wait()
     columns = []
     for q in range(7):
@@ -440,10 +446,23 @@
         )
 
     def sum_halves(level):
-        halves_copy(level).start()
+        if level > 0:
+            halves_copy(level).start()
 
     def sum_scatter(level):
         parts, halves, folded, gathered = buffers_of(level)[:4]
+        if level == 0:
+
+            @pl.loop(1, 32)
+            def _(step):
+                other, device = both_peer(step)
+                pltpu.make_async_remote_copy(
+                    parts.at[other], gathered_first.at[plane_index],
+                    sum_send.at[level, 1], sum_recv.at[level, 1], device, MESH,
+                ).start()
+
+            gathered_first[plane_index] = parts[plane_index]
+            return
         halves_copy(level).wait()
         mine = parts[pl.ds(16 * core, 16)].astype(F32)
         folded[...] = (mine + halves[...].astype(F32)).astype(BF16)
@@ -460,8 +479,11 @@
 
     def sum_across(level):
         _, _, folded, gathered, own, across, _ = buffers_of(level)
-        bulk_wait(folded, 15, sum_send.at[level, 1])
-        bulk_wait(gathered, 15, sum_recv.at[level, 1])
+        if level == 0:
+            folded = gathered = gathered_first
+        count = 31 if level == 0 else 15
+        bulk_wait(folded, count, sum_send.at[level, 1])
+        bulk_wait(gathered, count, sum_recv.at[level, 1])
         own[0] = jnp.sum(gathered[...].astype(F32), axis=0).astype(BF16)
 
         @pl.loop(1, 8)
@@ -480,29 +502,18 @@
         bulk_wait(across, 7, sum_recv.at[level, 2])
         total[plane_index] = jnp.sum(across[...].astype(F32), axis=0).astype(BF16)
 
-        @pl.loop(1, 16)
+        @pl.loop(1, 32)
         def _(step):
-            _, device = plane_peer(step)
+            _, device = both_peer(step)
             pltpu.make_async_remote_copy(
                 total.at[plane_index], total.at[plane_index],
                 sum_send.at[level, 3], sum_recv.at[level, 3], device, MESH,
             ).start()
 
-    def share_copy(level):
-        half = buffers_of(level)[6].at[pl.ds(16 * core, 16)]
-        return pltpu.make_async_remote_copy(
-            half, half, sum_send.at[level, 4], sum_recv.at[level, 4], twin, MESH
-        )
-
-    def sum_share(level):
-        total = buffers_of(level)[6]
-        bulk_wait(total, 15, sum_send.at[level, 3])
-        bulk_wait(total, 15, sum_recv.at[level, 3])
-        share_copy(level).start()
-
     def sum_finish(level):
         total = buffers_of(level)[6]
-        share_copy(level).wait()
+        bulk_wait(total, 31, sum_send.at[level, 3])
+        bulk_wait(total, 31, sum_recv.at[level, 3])
         if level in (0, 4):
             sums_small_ref[level // 4] = total[...].reshape(512, 128)
         else:
@@ -595,8 +606,6 @@
     bulk_wait(back_core, 7, block_send.at[2, 0])
     bulk_wait(back_rows, 7, block_recv.at[2, 0])
     grad_ref[...] = direct[...] + back_rows[...].reshape(NY, 128)
-    for level in (4, 3, 2, 1, 0):
-        sum_share(level)
     for level in (4, 3, 2, 1, 0):
         sum_finish(level)
 
@@ -650,6 +659,7 @@
             for shape in ((3, 16, 32, 128), (2, 16, 16, 128))
         ]
         + [
+            pltpu.VMEM((32, 16, 128), BF16),
             pltpu.VMEM((3, 1, 32, 128), BF16),
             pltpu.VMEM((2, 1, 16, 128), BF16),
             pltpu.VMEM((3, 8, 32, 128), BF16),

time: 75.6 us -> 78 us (1.032)
  Pallas kernels: 71 us -> 73.4 us
    pallas_call x1, Pallas kernels: 69 us -> 71.5 us  [main_call(): pl.pallas_call(main_kernel, out_shape=(jax.ShapeDtypeStruct((NY, 128), F3...]
where the time goes in v4:
time: 78 us; the launch traced here: 77.8 us
  Pallas kernels  73.4 us (94%)
  local copies, waits for them, and re-layouts  3.79 us (5%)
    pallas_call x1, Pallas kernels, main_call(): pl.pallas_call(main_kernel, out_shape=(jax.ShapeDtypeStruct((NY, 128), F3...  71.5 us
    unnamed x5, local copies, waits for them, and re-layouts  2.74 us
    pallas_call x1, Pallas kernels, finish_call(): pl.pallas_call(functools.partial(finish_kernel, 1.0 / math.sqrt(cells)),...  1.93 us

profile of v4, /device:TPU:1, one launch (start us, length us, event | category | flops | bytes accessed | tf_op | source)
XLA Modules:
  0.0 77.8 jit_solution(6266049449538922738)
XLA Ops:
  0.6 71.5 %step.1 = (f32[320,128]{1,0:T(8,128)}, bf16[3,1024,128]{2,1,0:T(8,128)(2,1)}, bf16[2,512,128]{2,1,0:T(8,128)(2,1)}) custom-call(f32[20,2,320]{2,1,0:T(2,128)} %bitcast.37, f32[16,2,320]{2,1,0:T(2,128)} %bitcast.38, bf16[2,512,20]{2,1,0:T(8,128)(2,1)} %constant.16.clone.refs_2_, bf16[2,512,16]{2,1,0:T(8,128)(2,1)} %constant.17.clone.refs_3_, ...), custom_call_target="tpu_custom_call" | custom-call | flops 8000000000 | bytes 20000000 | tf_op jit(solution)/shard_map/step/pallas_call | solution.py:619
  72.1 1.0 %copy.24 = f32[320,128]{0,1:T(8,128)S(1)} copy(f32[320,128]{1,0:T(8,128)} %get-tuple-element.14) | data formatting | bytes 327680 | tf_op jit(solution)/shard_map/step/pallas_call | solution.py:619
  73.2 0.7 copy.25
  73.8 0.0 copy-start
  73.8 1.1 %copy-done = bf16[3,1024,128]{2,1,0:T(8,128)(2,1)S(1)} copy-done((bf16[3,1024,128]{2,1,0:T(8,128)(2,1)S(1)}, bf16[3,1024,128]{2,1,0:T(8,128)(2,1)}, u32[]{:S(2)}) %copy-start) | copy-done | bytes 786456
  74.9 0.0 copy-start.1
  75.0 0.9 %copy-done.1 = bf16[2,512,128]{2,1,0:T(8,128)(2,1)S(1)} copy-done((bf16[2,512,128]{2,1,0:T(8,128)(2,1)S(1)}, bf16[2,512,128]{2,1,0:T(8,128)(2,1)}, u32[]{:S(2)}) %copy-start.1) | copy-done | bytes 262168
  75.9 1.9 %finish.1 = (f32[27,20,64]{2,1,0:T(8,128)}, f32[27,64,64]{2,1,0:T(8,128)}, f32[27,64,64]{2,1,0:T(8,128)}, f32[27,64,64]{2,1,0:T(8,128)}, f32[27,20,64]{2,1,0:T(8,128)}) custom-call(bf16[3,1024,128]{2,1,0:T(8,128)(2,1)S(1)} %copy-done, bf16[2,512,128]{2,1,0:T(8,128)(2,1)S(1)} %copy-done.1), custom_call_target="tpu_custom_call" | custom-call | tf_op jit(solution)/shard_map/finish/pallas_call | solution.py:728
  (1 shorter events, 0.0 us)
Async XLA Ops:
  73.8 1.1 %copy-start = (bf16[3,1024,128]{2,1,0:T(8,128)(2,1)S(1)}, bf16[3,1024,128]{2,1,0:T(8,128)(2,1)}, u32[]{:S(2)}) copy-start(bf16[3,1024,128]{2,1,0:T(8,128)(2,1)} %get-tuple-element.15.mid_ref) | copy-start | bytes 2359300
  74.9 0.9 %copy-start.1 = (bf16[2,512,128]{2,1,0:T(8,128)(2,1)S(1)}, bf16[2,512,128]{2,1,0:T(8,128)(2,1)}, u32[]{:S(2)}) copy-start(bf16[2,512,128]{2,1,0:T(8,128)(2,1)} %get-tuple-element.16.small_ref) | copy-start | bytes 786436

commit v5 on v4

--- a/solution.py
+++ b/solution.py
@@ -170,7 +170,7 @@
         pltpu.make_async_copy(source, target, table_sem.at[i])
         for i, (source, target) in enumerate(zip(sources, held))
     ]
-    for fetch in fetches[:5]:
+    for fetch in fetches[:12]:
         fetch.start()
 
     for i in range(3):
@@ -259,8 +259,6 @@
     coil[:, 0:NY] = (s_re * u_re - s_im * u_im).astype(BF16)
     coil[:, 384 : 384 + NY] = (s_re * u_im + s_im * u_re).astype(BF16)
     fetches[4].wait()
-    for fetch in fetches[5:]:
-        fetch.start()
     sub = lax.broadcasted_iota(jnp.int32, (8, 8, 128), 1) // 2
 
     @pl.loop(0, 8)
@@ -276,6 +274,11 @@
         extra = jnp.where(sub == 1, at_one, jnp.where(sub == 2, at_two, 0.0))
         packed = jnp.concatenate([body[:, 0:1], (body[:, 1] + extra)[:, None]], axis=1)
         message[pl.ds(step * 8, 8)] = packed.reshape(8, 16, 128).astype(BF16)
+
+    slot_z = lax.broadcasted_iota(jnp.int32, (24, 64, 128), 0) + (z_block * 8 - 8)
+    slot_y = lax.broadcasted_iota(jnp.int32, (24, 64, 128), 1) + (y_block * 40 - 8)
+    grid_ok = (slot_z >= 0) & (slot_z < NZ) & (slot_y >= 0) & (slot_y < NY)
+    inside[...] = jnp.where(grid_ok, 1.0, 0.0)
 
     def three_planes(buffer, first, count):
         pieces = [buffer[first + k : first + k + count].reshape(count * 64, 128) for k in (-1, 0, 1)]
@@ -310,14 +313,13 @@
             acts[level + 1, first : first + count] = value.astype(BF16).reshape(count, 64, 128)
             slopes[level, first : first + count] = slope.reshape(count, 64, 128)
 
+    for fetch in fetches[12:]:
+        fetch.start()
     fetches[5].wait()
     image = image_ref[...].astype(F32)
     cut(
         sum(dot(image[:, x, :].astype(BF16), places[x], TN) for x in range(2)), stage_image
     )
-    pl.semaphore_wait(barrier, 83)
-    exchange_start(message, arrived, 0)
-    blocks_send(stage_image, packed_image, 0)
     crossed = (((0,), (1,)), ((), ()))
     maps[...] = dot(s_high[0], es_ref[0], crossed) + dot(s_high[1], es_ref[1], crossed)
     rows_sum = jnp.zeros((NY, 128), F32)
@@ -341,11 +343,9 @@
                 ]
             taps_ref[level, tap] = jnp.concatenate(pieces, axis=0).astype(BF16)
 
-    slot_z = lax.broadcasted_iota(jnp.int32, (24, 64, 128), 0) + (z_block * 8 - 8)
-    slot_y = lax.broadcasted_iota(jnp.int32, (24, 64, 128), 1) + (y_block * 40 - 8)
-    grid_ok = (slot_z >= 0) & (slot_z < NZ) & (slot_y >= 0) & (slot_y < NY)
-    inside[...] = jnp.where(grid_ok, 1.0, 0.0)
-
+    pl.semaphore_wait(barrier, 83)
+    exchange_start(message, arrived, 0)
+    blocks_send(stage_image, packed_image, 0)
     fetches[12].wait()
     columns = []
     for q in range(7):
@@ -501,19 +501,35 @@
         bulk_wait(across, 7, sum_send.at[level, 2])
         bulk_wait(across, 7, sum_recv.at[level, 2])
         total[plane_index] = jnp.sum(across[...].astype(F32), axis=0).astype(BF16)
-
-        @pl.loop(1, 32)
+        peer = both_peer if level == 0 else plane_peer
+
+        @pl.loop(1, 32 if level == 0 else 16)
         def _(step):
-            _, device = both_peer(step)
+            _, device = peer(step)
             pltpu.make_async_remote_copy(
                 total.at[plane_index], total.at[plane_index],
                 sum_send.at[level, 3], sum_recv.at[level, 3], device, MESH,
             ).start()
 
+    def share_copy(level):
+        half = buffers_of(level)[6].at[pl.ds(16 * core, 16)]
+        return pltpu.make_async_remote_copy(
+            half, half, sum_send.at[level, 4], sum_recv.at[level, 4], twin, MESH
+        )
+
+    def sum_share(level):
+        total = buffers_of(level)[6]
+        bulk_wait(total, 15, sum_send.at[level, 3])
+        bulk_wait(total, 15, sum_recv.at[level, 3])
+        share_copy(level).start()
+
     def sum_finish(level):
         total = buffers_of(level)[6]
-        bulk_wait(total, 31, sum_send.at[level, 3])
-        bulk_wait(total, 31, sum_recv.at[level, 3])
+        if level == 0:
+            bulk_wait(total, 31, sum_send.at[level, 3])
+            bulk_wait(total, 31, sum_recv.at[level, 3])
+        else:
+            share_copy(level).wait()
         if level in (0, 4):
             sums_small_ref[level // 4] = total[...].reshape(512, 128)
         else:
@@ -606,6 +622,8 @@
     bulk_wait(back_core, 7, block_send.at[2, 0])
     bulk_wait(back_rows, 7, block_recv.at[2, 0])
     grad_ref[...] = direct[...] + back_rows[...].reshape(NY, 128)
+    for level in (4, 3, 2, 1):
+        sum_share(level)
     for level in (4, 3, 2, 1, 0):
         sum_finish(level)
 

time: 78 us -> 75.4 us (0.967)
  Pallas kernels: 73.4 us -> 70.8 us
    pallas_call x1, Pallas kernels: 71.5 us -> 68.8 us  [main_call(): pl.pallas_call(main_kernel, out_shape=(jax.ShapeDtypeStruct((NY, 128), F3...]
where the time goes in v5:
time: 75.4 us; the launch traced here: 75.2 us
  Pallas kernels  70.8 us (94%)
  local copies, waits for them, and re-layouts  3.79 us (5%)
    pallas_call x1, Pallas kernels, main_call(): pl.pallas_call(main_kernel, out_shape=(jax.ShapeDtypeStruct((NY, 128), F3...  68.8 us
    unnamed x5, local copies, waits for them, and re-layouts  2.74 us
    pallas_call x1, Pallas kernels, finish_call(): pl.pallas_call(functools.partial(finish_kernel, 1.0 / math.sqrt(cells)),...  1.93 us

profile of v5, /device:TPU:1, one launch (start us, length us, event | category | flops | bytes accessed | tf_op | source)
XLA Modules:
  0.0 75.2 jit_solution(6331622422623414489)
XLA Ops:
  0.6 68.8 %step.1 = (f32[320,128]{1,0:T(8,128)}, bf16[3,1024,128]{2,1,0:T(8,128)(2,1)}, bf16[2,512,128]{2,1,0:T(8,128)(2,1)}) custom-call(f32[20,2,320]{2,1,0:T(2,128)} %bitcast.37, f32[16,2,320]{2,1,0:T(2,128)} %bitcast.38, bf16[2,512,20]{2,1,0:T(8,128)(2,1)} %constant.16.clone.refs_2_, bf16[2,512,16]{2,1,0:T(8,128)(2,1)} %constant.17.clone.refs_3_, ...), custom_call_target="tpu_custom_call" | custom-call | flops 8000000000 | bytes 20000000 | tf_op jit(solution)/shard_map/step/pallas_call | solution.py:637
  69.5 1.0 %copy.24 = f32[320,128]{0,1:T(8,128)S(1)} copy(f32[320,128]{1,0:T(8,128)} %get-tuple-element.14) | data formatting | bytes 327680 | tf_op jit(solution)/shard_map/step/pallas_call | solution.py:637
  70.5 0.7 copy.25
  71.2 0.0 copy-start
  71.2 1.1 %copy-done = bf16[3,1024,128]{2,1,0:T(8,128)(2,1)S(1)} copy-done((bf16[3,1024,128]{2,1,0:T(8,128)(2,1)S(1)}, bf16[3,1024,128]{2,1,0:T(8,128)(2,1)}, u32[]{:S(2)}) %copy-start) | copy-done | bytes 786456
  72.3 0.0 copy-start.1
  72.3 0.9 %copy-done.1 = bf16[2,512,128]{2,1,0:T(8,128)(2,1)S(1)} copy-done((bf16[2,512,128]{2,1,0:T(8,128)(2,1)S(1)}, bf16[2,512,128]{2,1,0:T(8,128)(2,1)}, u32[]{:S(2)}) %copy-start.1) | copy-done | bytes 262168
  73.3 1.9 %finish.1 = (f32[27,20,64]{2,1,0:T(8,128)}, f32[27,64,64]{2,1,0:T(8,128)}, f32[27,64,64]{2,1,0:T(8,128)}, f32[27,64,64]{2,1,0:T(8,128)}, f32[27,20,64]{2,1,0:T(8,128)}) custom-call(bf16[3,1024,128]{2,1,0:T(8,128)(2,1)S(1)} %copy-done, bf16[2,512,128]{2,1,0:T(8,128)(2,1)S(1)} %copy-done.1), custom_call_target="tpu_custom_call" | custom-call | tf_op jit(solution)/shard_map/finish/pallas_call | solution.py:746
  (1 shorter events, 0.0 us)
Async XLA Ops:
  71.2 1.1 %copy-start = (bf16[3,1024,128]{2,1,0:T(8,128)(2,1)S(1)}, bf16[3,1024,128]{2,1,0:T(8,128)(2,1)}, u32[]{:S(2)}) copy-start(bf16[3,1024,128]{2,1,0:T(8,128)(2,1)} %get-tuple-element.15.mid_ref) | copy-start | bytes 2359300
  72.3 0.9 %copy-start.1 = (bf16[2,512,128]{2,1,0:T(8,128)(2,1)S(1)}, bf16[2,512,128]{2,1,0:T(8,128)(2,1)}, u32[]{:S(2)}) copy-start(bf16[2,512,128]{2,1,0:T(8,128)(2,1)} %get-tuple-element.16.small_ref) | copy-start | bytes 786436
